TPU v7x, 32 devices: a whole 2x2x4 slice. The times are simulated.
32 devices in a mesh: seq: 8 (over z, y), mp: 4 (over x, core).
Axes of the slice: x: 2, y: 2, z: 4, core: 2. Of those that a mesh axis runs over, the one named last changes fastest.
Arguments:
- token_ids: int32 [2, 1024], P(None, 'seq'), may hold values from 0 to 511, as said below
- pair_mask: int32 [1024], P('seq'), may hold values from 0 to 1
- embed_table: bfloat16 [512, 3, 4096], P(None, None, 'mp'), may hold values from -6 to 6
- conv_filter: bfloat16 [256, 128], P('mp'), may hold values from -0.9 to 1
- w_out: bfloat16 [4096, 4096], P('mp'), may hold values from -0.09375 to 0.09375
- w_qkv: bfloat16 [3, 32, 128, 128], P(None, 'mp'), may hold values from -0.61871843 to 0.61871843
Outputs:
- gram: float32 [32, 128, 128], P('mp', 'seq')
Inputs may be any that keep to these rules, and one draw needn't show every extreme that they name: `token_ids`: row 1 equals row 0 at about half of the positions.
All inputs are finite; a program needn't handle non-finite values.
Results may differ from a plain program's by a relative error of at most 0.0074.
Values may be sent and summed in bfloat16 or wider, within the bound.
No kernel may reach another device: no remote copies, remote signals or barrier semaphores. Data moves between devices by JAX's collectives and lax.ppermute only.
A program may use at most 128 MiB of HBM per device.

v0:
```python
import math

import jax
import jax.numpy as jnp
from jax import lax
from jax.sharding import PartitionSpec as P

MASKED_SCORE = -1e30


def from_behind(value, axis, steps):
    count = lax.axis_size(axis)
    initial, last = (max(0, -steps), min(count, count - steps))
    return lax.ppermute(value, axis, [(source, source + steps) for source in range(initial, last)])


def lookup(token_ids, embed_table):
    vocab_size = embed_table.shape[0]
    onehot = (
        token_ids[:, :, None] == jnp.arange(vocab_size, dtype=jnp.int32)[None, None, :]
    ).astype(jnp.bfloat16)
    flat_table = embed_table.reshape(vocab_size, -1)
    features = jnp.einsum("stv,vc->stc", onehot, flat_table, preferred_element_type=jnp.float32)
    return features.astype(jnp.bfloat16).reshape(
        token_ids.shape[0], token_ids.shape[1], 3, embed_table.shape[2]
    )


def toeplitz(conv_filter):
    tap_count = conv_filter.shape[1]
    out_index = jnp.arange(tap_count, dtype=jnp.int32)[:, None, None]
    in_index = jnp.arange(2 * tap_count, dtype=jnp.int32)[None, :, None]
    lag_index = jnp.arange(tap_count, dtype=jnp.int32)[None, None, :]
    selector = (lag_index == out_index + tap_count - in_index).astype(jnp.bfloat16)
    return jnp.einsum(
        "gj,tsj->gts", conv_filter, selector, preferred_element_type=jnp.float32
    ).astype(jnp.bfloat16)


def project(row_block, weight):
    return jnp.einsum(
        "sthd,hde->sthe", row_block, weight, preferred_element_type=jnp.float32
    ).astype(jnp.bfloat16)


def body(token_ids, pair_mask, embed_table, conv_filter, w_out, w_qkv):
    local_len = token_ids.shape[1]
    channels = embed_table.shape[2]
    filters, tap_count = conv_filter.shape
    group_width = channels // filters
    head_count, head_dim = (w_qkv.shape[1], w_qkv.shape[2])
    my_index = lax.axis_index("seq")
    score_scale = 1.0 / math.sqrt(head_dim)
    features = lookup(token_ids, embed_table)
    gated = (features[:, :, 1].astype(jnp.float32) * features[:, :, 2].astype(jnp.float32)).astype(
        jnp.bfloat16
    )
    before = from_behind(gated, "seq", 1)
    window = jnp.concatenate([before, gated], axis=1)
    blocks = local_len // tap_count
    lower_half = window[:, :local_len].reshape(2, blocks, tap_count, filters, group_width)
    upper_half = window[:, tap_count:].reshape(2, blocks, tap_count, filters, group_width)
    framed = jnp.concatenate([lower_half, upper_half], axis=2)
    convolved = jnp.einsum(
        "gts,bnsgc->bntgc", toeplitz(conv_filter), framed, preferred_element_type=jnp.float32
    )
    hyena_out = (
        features[:, :, 0].astype(jnp.float32) * convolved.reshape(2, local_len, channels)
    ).astype(jnp.bfloat16)
    partial_value = jnp.dot(
        hyena_out.reshape(2 * local_len, channels), w_out, preferred_element_type=jnp.float32
    )
    partial_value = partial_value.reshape(2, local_len, w_out.shape[1])
    mixed_out = lax.psum_scatter(partial_value, "mp", scatter_dimension=2, tiled=True).astype(
        jnp.bfloat16
    )
    mixed_heads = mixed_out.reshape(2, local_len, head_count, head_dim)
    queries = project(mixed_heads, w_qkv[0])
    query_pos = my_index * local_len + jnp.arange(local_len, dtype=jnp.int32)

    def fold_block(running, key_rows, value_rows, offset):
        row_max, row_sum, weighted = running
        scores = (
            jnp.einsum("sqhe,skhe->shqk", queries, key_rows, preferred_element_type=jnp.float32)
            * score_scale
        )
        key_pos = offset + jnp.arange(key_rows.shape[1], dtype=jnp.int32)
        causal = key_pos[None, :] <= query_pos[:, None]
        new_max = jnp.maximum(row_max, jnp.max(jnp.where(causal, scores, MASKED_SCORE), axis=-1))
        weights = jnp.where(causal, jnp.exp(scores - new_max[..., None]), 0.0)
        rescale = jnp.exp(row_max - new_max)
        row_sum = row_sum * rescale + jnp.sum(weights, axis=-1)
        update = jnp.einsum(
            "shqk,skhe->shqe",
            weights.astype(jnp.bfloat16),
            value_rows,
            preferred_element_type=jnp.float32,
        )
        weighted = weighted * rescale[..., None] + update
        return (new_max, row_sum, weighted)

    def sweep_keys(running, pieces, begin_at, expand):
        row_count = pieces[0].shape[1]
        block_rows = 1024 if row_count > 1024 and row_count % 1024 == 0 else row_count
        if block_rows == row_count:
            key_rows, value_rows = expand(pieces)
            return fold_block(running, key_rows, value_rows, begin_at)

        def advance(block_index, state_now):
            offset = block_index * block_rows
            sliced = tuple(
                (lax.dynamic_slice_in_dim(member, offset, block_rows, 1) for member in pieces)
            )
            key_rows, value_rows = expand(sliced)
            return fold_block(state_now, key_rows, value_rows, begin_at + offset)

        return lax.fori_loop(0, row_count // block_rows, advance, running)

    initial = (
        jnp.full((2, head_count, local_len), MASKED_SCORE, jnp.float32),
        jnp.zeros((2, head_count, local_len), jnp.float32),
        jnp.zeros((2, head_count, local_len, head_dim), jnp.float32),
    )
    key_heads = project(mixed_heads, w_qkv[1])
    value_heads = project(mixed_heads, w_qkv[2])

    def expand_pair(pieces):
        return (pieces[0], pieces[1])

    final = sweep_keys(
        initial,
        (
            lax.all_gather(key_heads, "seq", axis=1, tiled=True),
            lax.all_gather(value_heads, "seq", axis=1, tiled=True),
        ),
        jnp.int32(0),
        expand_pair,
    )
    row_max, row_sum, weighted = final
    attended = weighted / row_sum[..., None]
    difference = (attended[0] - attended[1]).astype(jnp.bfloat16)
    mask_float = pair_mask.astype(jnp.bfloat16)
    kept_rows = difference * mask_float[None, :, None]
    partial_gram = jnp.einsum(
        "hte,htf->hef", kept_rows, difference, preferred_element_type=jnp.float32
    )
    gram_sum = lax.psum_scatter(partial_gram, "seq", scatter_dimension=1, tiled=True)
    kept_count = lax.psum(jnp.sum(pair_mask.astype(jnp.float32)), "seq")
    return gram_sum / jnp.maximum(kept_count, 1.0)


def solution(mesh):
    in_specs = (
        P(None, "seq"),
        P("seq"),
        P(None, None, "mp"),
        P("mp", None),
        P("mp", None),
        P(None, "mp", None, None),
    )
    out_specs = P("mp", "seq", None)
    return jax.shard_map(body, mesh=mesh, in_specs=in_specs, out_specs=out_specs, check_vma=False)
```

profile of v0, /device:TPU:0, one launch (start us, length us, event | category | flops | bytes accessed | tf_op | source)
XLA Modules:
  0.0 315.9 jit_solution(3529989364438648276)
XLA Ops:
  6.5 0.0 copy-start
  6.5 0.0 copy-start.3
  6.5 0.0 reduce-scatter.3.cloned.1.call-start
  6.5 3.2 %copy.9 = bf16[512,3,1024]{0,2,1:T(8,128)(2,1)S(1)} copy(bf16[512,3,1024]{2,0,1:T(8,128)(2,1)} %param.8) | data formatting | bytes 6291456 | tf_op args[2]
  9.8 0.0 copy-done.3
  9.8 2.2 convolution_convert_fusion
  12.0 1.9 copy.11
  13.9 0.1 multiply_convert_fusion
  14.0 0.2 copy.12
  14.3 4.9 %collective-permute-start = (bf16[2,128,1024]{2,1,0:T(8,128)(2,1)S(1)}, bf16[2,128,1024]{2,1,0:T(8,128)(2,1)S(1)}, u32[]{:S(2)}, u32[]{:S(2)}) collective-permute-start(bf16[2,128,1024]{2,1,0:T(8,128)(2,1)S(1)} %bitcast.93), channel_id=1, source_target_pairs={{0,4},{4,8},{8,12},{12,16},{16,20},{20,24},{24,28},{1,5},{5,9},{9,... | collective-permute-start | bytes 1572872 | tf_op jit(solution)/shard_map/ppermute | solution.py:14
  19.2 0.1 iota_subtract_fusion
  19.3 0.0 copy-done
  19.3 9.1 %fusion = bf16[128,256,64]{1,2,0:T(8,128)(2,1)} fusion(s32[128,256]{1,0:T(8,128)S(1)} %iota_subtract_fusion, bf16[64,128]{1,0:T(8,128)(2,1)S(1)} %copy-done), kind=kOutput, calls=%fused_computation.1 | convolution fusion | flops 541065216 | bytes 4341760 | tf_op jit(solution)/shard_map/gj,tsj->gts/dot_general | solution.py:35
  28.4 1.9 collective-permute-done
  30.3 0.3 copy.13
  30.6 4.6 %fusion.15 = f32[2,1,128,64,16]{2,4,0,3,1:T(8,128)S(1)} fusion(bf16[128,256,64]{1,2,0:T(8,128)(2,1)} %fusion, bf16[2,1,128,64,16]{2,4,3,0,1:T(8,128)(2,1)S(1)} %bitcast.92, bf16[2,1,128,64,16]{2,4,3,0,1:T(8,128)(2,1)S(1)} %bitcast.94), kind=kOutput, calls=%fused_computation.18 | convolution fusion | flops 136314880 | bytes 6291456 | tf_op jit(solution)/shard_map/gts,bnsgc->bntgc/dot_general | solution.py:64
  35.1 0.1 copy.16
  35.2 7.7 %fusion.1 = f32[2,128,4096]{2,1,0:T(8,128)} fusion(bf16[1024,4096]{1,0:T(8,128)(2,1)} %param.10, f32[2,128,1024]{1,2,0:T(8,128)S(1)} %bitcast.91, bf16[2,128,3,1024]{1,3,2,0:T(8,128)(2,1)S(1)} %bitcast.90), kind=kOutput, calls=%fused_computation.2 | convolution fusion | flops 2148270080 | bytes 14155776 | tf_op jit(solution)/shard_map/dot_general | solution.py:70
  42.9 0.0 copy-start.2
  42.9 0.0 copy-start.4
  42.9 0.0 reduce-scatter.3.cloned.1.call-update
  43.0 0.0 all-gather.3.cloned.1.call-start
  43.0 46.8 %reduce-scatter.3.cloned.1.call-done = f32[2,128,1024]{2,1,0:T(8,128)} async-done(((f32[2,128,4096]{2,1,0:T(8,128)}), f32[2,128,1024]{2,1,0:T(8,128)}) %reduce-scatter.3.cloned.1.call-update) | async-done | bytes 1048592 | tf_op jit(solution)/shard_map/reduce_scatter | solution.py:74
  89.8 0.0 copy-done.2
  89.8 0.0 copy-start.1
  89.8 2.4 fusion.23
  92.3 0.0 all-gather.3.cloned.1.call-update
  92.3 0.0 all-gather.5.cloned.1.call-start
  92.3 2.3 fusion.24
  94.6 0.0 all-gather.5.cloned.1.call-update
  94.7 0.2 reduce-scatter.5.cloned.1.call-start
  94.9 0.0 copy-done.4
  94.9 0.1 iota_compare_fusion.3
  95.1 70.7 %all-gather.3.cloned.1.call-done = bf16[2,1024,8,128]{3,1,2,0:T(8,128)(2,1)} async-done(((bf16[2,128,8,128]{3,1,2,0:T(8,128)(2,1)}), bf16[2,1024,8,128]{3,1,2,0:T(8,128)(2,1)}) %all-gather.3.cloned.1.call-update) | async-done | bytes 4194320 | tf_op jit(solution)/shard_map/all_gather | solution.py:133
  165.8 0.0 copy-done.1
  165.8 7.1 %select_reduce_fusion = (f32[2,8,128]{2,1,0:T(8,128)S(1)}, f32[2,8,128,1024]{3,2,1,0:T(8,128)}) fusion(pred[128,1024]{1,0:T(8,128)(4,1)S(1)} %iota_compare_fusion.3, bf16[2,1024,8,128]{3,1,2,0:T(8,128)(2,1)} %all-gather.3.cloned.1.call-done, bf16[3,8,128,128]{3,2,1,0:T(8,128)(2,1)S(1)} %copy-done.2, f32[2,128,1024]{2,1,0:T(8,128)S(1)} %copy-done.1), kind=kOutput, calls=%fused_computation.6 | convolution fusion | flops 610793472 | bytes 14032896 | tf_op jit(solution)/shard_map/sqhe,skhe->shqk/dot_general | solution.py:84
  173.0 5.1 %fusion.4 = f32[2,8,128]{2,1,0:T(8,128)S(1)} fusion(f32[2,8,128,1024]{3,2,1,0:T(8,128)} %get-tuple-element.8, f32[2,8,128]{2,1,0:T(8,128)S(1)} %broadcast_maximum_fusion, pred[128,1024]{1,0:T(8,128)(4,1)S(1)} %iota_compare_fusion.3), kind=kLoop, calls=%fused_computation.8 | loop fusion | flops 8386560 | bytes 8536064 | tf_op jit(solution)/shard_map/reduce_sum | solution.py:92
  178.1 61.9 %all-gather.5.cloned.1.call-done = bf16[2,1024,8,128]{3,1,2,0:T(8,128)(2,1)} async-done(((bf16[2,128,8,128]{3,1,2,0:T(8,128)(2,1)}), bf16[2,1024,8,128]{3,1,2,0:T(8,128)(2,1)}) %all-gather.5.cloned.1.call-update) | async-done | bytes 4194320 | tf_op jit(solution)/shard_map/all_gather | solution.py:134
  239.9 5.9 %fusion.28 = f32[2,8,128,128]{3,2,1,0:T(8,128)S(1)} fusion(bf16[2,1024,8,128]{3,1,2,0:T(8,128)(2,1)} %all-gather.5.cloned.1.call-done, f32[2,8,128,1024]{3,2,1,0:T(8,128)} %get-tuple-element.8, f32[2,8,128]{2,1,0:T(8,128)S(1)} %broadcast_maximum_fusion, pred[128,1024]{1,0:T(8,128)(4,1)S(1)} %iota_compare_fusion.3, f32[2,8,128]{2,1,0:T(8,128)S(1)} %get-tuple-element.6, ...), kind=kOutput, calls=%fused_computation.33 | convolution fusion | flops 545783808 | bytes 13787136 | tf_op jit(solution)/shard_map/shqk,skhe->shqe/dot_general | solution.py:93
  245.9 1.1 fusion.41
  247.0 0.0 reduce-scatter.5.cloned.1.call-update
  247.0 0.6 convert_reduce_fusion
  247.6 19.3 %psum.7 = f32[]{:T(128)} all-reduce(f32[]{:T(128)} %convert_reduce_fusion), channel_id=1, replica_groups=mesh['seq'=8,'mp'=4] {'seq'}, use_global_device_ids=true, to_apply=%region_5.6 | all-reduce | flops 1 | bytes 8 | tf_op jit(solution)/shard_map/psum | solution.py:148
  267.6 40.2 %reduce-scatter.5.cloned.1.call-done = f32[8,16,128]{2,1,0:T(8,128)} async-done(((f32[8,128,128]{2,1,0:T(8,128)}), f32[8,16,128]{2,1,0:T(8,128)}) %reduce-scatter.5.cloned.1.call-update) | async-done | bytes 65552 | tf_op jit(solution)/shard_map/reduce_scatter | solution.py:147
  307.8 1.5 broadcast_divide_fusion
  (5 shorter events, 0.0 us)
Async XLA Ops:
  6.5 12.7 %copy-start = (bf16[64,128]{1,0:T(8,128)(2,1)S(1)}, bf16[64,128]{1,0:T(8,128)(2,1)}, u32[]{:S(2)}) copy-start(bf16[64,128]{1,0:T(8,128)(2,1)} %param.9) | copy-start | bytes 49156
  6.5 3.2 %copy-start.3 = (s32[2,128]{1,0:T(2,128)S(1)}, s32[2,128]{1,0:T(2,128)}, u32[]{:S(2)}) copy-start(s32[2,128]{1,0:T(2,128)} %param.6) | copy-start | bytes 3076
  6.5 83.3 %reduce-scatter.3.cloned.1.call-start = ((), (), s32[]{:S(2)}) async-start(), calls=%async_computation.2 | async-start | bytes 5242880 | tf_op jit(solution)/shard_map/reduce_scatter | solution.py:74
  14.3 16.0 %collective-permute-start = (bf16[2,128,1024]{2,1,0:T(8,128)(2,1)S(1)}, bf16[2,128,1024]{2,1,0:T(8,128)(2,1)S(1)}, u32[]{:S(2)}, u32[]{:S(2)}) collective-permute-start(bf16[2,128,1024]{2,1,0:T(8,128)(2,1)S(1)} %bitcast.93), channel_id=1, source_target_pairs={{0,4},{4,8},{8,12},{12,16},{16,20},{20,24},{24,28},{1,5},{5,9},{9,... | collective-permute-start | bytes 1572872 | tf_op jit(solution)/shard_map/ppermute | solution.py:14
  42.9 46.9 %copy-start.2 = (bf16[3,8,128,128]{3,2,1,0:T(8,128)(2,1)S(1)}, bf16[3,8,128,128]{3,2,1,0:T(8,128)(2,1)}, u32[]{:S(2)}) copy-start(bf16[3,8,128,128]{3,2,1,0:T(8,128)(2,1)} %param.11) | copy-start | bytes 2359300
  42.9 52.0 %copy-start.4 = (s32[128]{0:T(128)S(1)}, s32[128]{0:T(128)}, u32[]{:S(2)}) copy-start(s32[128]{0:T(128)} %param.7) | copy-start | bytes 1540
  43.0 122.9 %all-gather.3.cloned.1.call-start = ((), (), s32[]{:S(2)}) async-start(), calls=%async_computation.3 | async-start | bytes 4718592 | tf_op jit(solution)/shard_map/all_gather | solution.py:133
  89.8 76.0 %copy-start.1 = (f32[2,128,1024]{2,1,0:T(8,128)S(1)}, f32[2,128,1024]{2,1,0:T(8,128)}, u32[]{:S(2)}) copy-start(f32[2,128,1024]{2,1,0:T(8,128)} %reduce-scatter.3.cloned.1.call-done) | copy-start | bytes 3145732
  92.3 147.6 %all-gather.5.cloned.1.call-start = ((), (), s32[]{:S(2)}) async-start(), calls=%async_computation.4 | async-start | bytes 4718592 | tf_op jit(solution)/shard_map/all_gather | solution.py:134
  94.7 213.2 %reduce-scatter.5.cloned.1.call-start = ((), (), s32[]{:S(2)}) async-start(), calls=%async_computation.5 | async-start | bytes 589824 | tf_op jit(solution)/shard_map/reduce_scatter | solution.py:147
Sparse Core Ops, SparseCore 0:
  43.1 46.7 reduce-scatter.2
  92.4 73.3 all-gather.2
  168.2 71.6 all-gather.4
  247.2 60.6 reduce-scatter.4
where the time goes:
time: 316 us
  waiting for transfers between devices  222 us (70%)
  matrix products  42.6 us (13%)
  blocking collectives  19.3 us (6%)
  between operations  13.9 us (4%)
  other arithmetic  7.54 us (2%)
  local copies, waits for them, and re-layouts  5.7 us (2%)
  starting transfers between devices  5.21 us (2%)
    all_gather x1, waiting for transfers between devices, body(): lax.all_gather(key_heads, 'seq', axis=1, tiled=True)  70.7 us
    all_gather x1, waiting for transfers between devices, body(): lax.all_gather(value_heads, 'seq', axis=1, tiled=True)  61.9 us
    reduce_scatter x1, waiting for transfers between devices, body(): lax.psum_scatter(partial_value, 'mp', scatter_dimension=2, tiled=True)  46.8 us
    reduce_scatter x1, waiting for transfers between devices, body(): lax.psum_scatter(partial_gram, 'seq', scatter_dimension=1, tiled=True)  40.2 us
    psum x1, blocking collectives, body(): kept_count = lax.psum(jnp.sum(pair_mask.astype(jnp.float32)), 'seq')  19.3 us
    dot_general x1, matrix products, toeplitz(): jnp.einsum('gj,tsj->gts', conv_filter, selector, preferred_element_type=j...  9.14 us
    dot_general x1, matrix products, body(): jnp.dot(hyena_out.reshape(2 * local_len, channels), w_out, preferred_elem...  7.71 us
    dot_general x1, matrix products, fold_block(): jnp.einsum('sqhe,skhe->shqk', queries, key_rows, preferred_element_type=j...  7.14 us
  transfers between devices with their start and end apart: 5, of which 5 were waited for; matrix products, arithmetic and copies ran while one was open for 8% of the time, Pallas kernels for 0%

commit v1 on v0

v1 whole, which is shorter than its diff:
```python
import functools
import math

import jax
import jax.numpy as jnp
from jax import lax
from jax.experimental import pallas as pl
from jax.experimental.pallas import tpu as pltpu
from jax.sharding import PartitionSpec as P

MASKED_SCORE = -1e30
VMEM_BYTES = 24 * 1024 * 1024
TABLES_VMEM_BYTES = 48 * 1024 * 1024
WHOLE = pl.BlockSpec(memory_space=pltpu.VMEM)
IN_HBM = pl.BlockSpec(memory_space=pltpu.HBM)


def params(limit=VMEM_BYTES):
    return pltpu.CompilerParams(vmem_limit_bytes=limit)


def bits_of(count):
    width = count.bit_length() - 1
    assert 1 << width == count
    return width


def swap(value, axis, turn):
    count = lax.axis_size(axis)
    return lax.ppermute(value, axis, [(i, i ^ turn) for i in range(count)])


def gather_small(block, axis):
    index = lax.axis_index(axis)
    held = block[None]
    bits = list(range(bits_of(lax.axis_size(axis))))
    for group in [bits[i : i + 2] for i in range(0, len(bits), 2)]:
        pieces = []
        for turn in range(1 << len(group)):
            mask = turn << group[0]
            pieces.append(held if turn == 0 else swap(held, axis, mask))
        for place, bit in enumerate(group):
            upper = ((index >> bit) & 1) == 1
            pieces = [
                jnp.where(upper, pieces[turn ^ (1 << place)], pieces[turn])
                for turn in range(len(pieces))
            ]
        held = jnp.concatenate(pieces, 0)
    return held


def head_here(seq_count, local_heads):
    return lax.axis_index("seq") // (seq_count // local_heads)


def tables_kernel(
    order, local_heads, seq_count, head_dim, embed_ref, w_out_ref, table_ref, weight_ref, planes,
    columns, plane_sems, column_sems
):
    _, vocab, channels = embed_ref.shape
    chunk = planes.shape[2]
    head = head_here(seq_count, local_heads)
    mp_index = lax.axis_index("mp")
    plane_copies = []
    for c in range(vocab // chunk):
        rows = pl.ds(c * chunk, chunk)
        plane_copies.append(
            [
                pltpu.make_async_copy(embed_ref.at[i, rows], planes.at[i, c], plane_sems.at[i, c])
                for i in range(3)
            ]
        )
    column_copies = []
    for p, turn in enumerate(order):
        first = pl.multiple_of(((mp_index ^ turn) * local_heads + head) * head_dim, head_dim)
        column_copies.append(
            pltpu.make_async_copy(
                w_out_ref.at[:, pl.ds(first, head_dim)], columns.at[p], column_sems.at[p]
            )
        )
    for copy in column_copies:
        copy.start()
    for trio in plane_copies:
        for copy in trio:
            copy.start()
    for p, copy in enumerate(column_copies):
        copy.wait()
        weight_ref[p * head_dim : (p + 1) * head_dim, :] = columns[p].T
    for c, trio in enumerate(plane_copies):
        for copy in trio:
            copy.wait()
        cols = slice(c * chunk, (c + 1) * chunk)
        gated = planes[1, c].astype(jnp.float32) * planes[2, c].astype(jnp.float32)
        table_ref[0:channels, cols] = gated.astype(jnp.bfloat16).T
        table_ref[channels : 2 * channels, cols] = planes[0, c].T


def make_tables(order, seq_count, local_heads, head_dim, embed_rows, w_out):
    _, vocab, channels = embed_rows.shape
    count = len(order)
    chunk = 128
    return pl.pallas_call(
        functools.partial(tables_kernel, order, local_heads, seq_count, head_dim),
        out_shape=[
            jax.ShapeDtypeStruct((2 * channels, vocab), jnp.bfloat16),
            jax.ShapeDtypeStruct((count * head_dim, w_out.shape[0]), jnp.bfloat16),
        ],
        in_specs=[IN_HBM, IN_HBM],
        out_specs=[WHOLE] * 2,
        scratch_shapes=[
            pltpu.VMEM((3, vocab // chunk, chunk, channels), jnp.bfloat16),
            pltpu.VMEM((count, w_out.shape[0], head_dim), jnp.bfloat16),
            pltpu.SemaphoreType.DMA((3, vocab // chunk)),
            pltpu.SemaphoreType.DMA((count,)),
        ],
        compiler_params=params(TABLES_VMEM_BYTES),
        cost_estimate=pl.CostEstimate(
            flops=4 * vocab * channels, bytes_accessed=8 * 1024 * 1024, transcendentals=0
        ),
    )(embed_rows, w_out)


def toeplitz_kernel(filter_ref, toeplitz_ref):
    filters, taps = filter_ref.shape
    row = lax.broadcasted_iota(jnp.int32, (taps, taps), 0)
    col = lax.broadcasted_iota(jnp.int32, (taps, taps), 1)
    for g in range(filters):
        spread = jnp.broadcast_to(filter_ref[g : g + 1, :].astype(jnp.float32), (taps, taps))
        rolled = pltpu.roll(spread, 0, 1, stride=1, stride_axis=0)
        toeplitz_ref[g, 0:taps, :] = jnp.where(col < row, rolled, 0.0).astype(jnp.bfloat16)
        toeplitz_ref[g, taps : 2 * taps, :] = jnp.where(col >= row, rolled, 0.0).astype(
            jnp.bfloat16
        )


def make_toeplitz(conv_filter):
    filters, taps = conv_filter.shape
    return pl.pallas_call(
        toeplitz_kernel,
        out_shape=jax.ShapeDtypeStruct((filters, 2 * taps, taps), jnp.bfloat16),
        in_specs=[WHOLE],
        out_specs=WHOLE,
        compiler_params=params(),
        cost_estimate=pl.CostEstimate(
            flops=4 * filters * taps * taps,
            bytes_accessed=4 * filters * taps * taps,
            transcendentals=0,
        ),
    )(conv_filter)


def hyena_kernel(
    which,
    group,
    ids_ref,
    table_ref,
    toeplitz_ref,
    weight_ref,
    _,
    out_ref,
    pass_ref,
    send_ref,
    feat,
    last,
):
    taps = ids_ref.shape[2]
    channels2, vocab = table_ref.shape
    channels = channels2 // 2
    filters = toeplitz_ref.shape[0]
    blocks = feat.shape[1] // taps
    step_index = pl.program_id(0)

    @pl.when(step_index == 0)
    def _():
        last[...] = jnp.zeros_like(last)

    entry = lax.broadcasted_iota(jnp.int32, (vocab, taps), 0)
    step = 2 if blocks % 2 == 0 else 1
    for b in range(0, blocks, step):
        hot = []
        for j in range(step):
            place = step_index * blocks + b + j
            tokens = jnp.broadcast_to(ids_ref[place, which : which + 1, :], (vocab, taps))
            hot.append((entry == tokens).astype(jnp.float32).astype(jnp.bfloat16))
        feat[:, b * taps : (b + step) * taps] = jnp.dot(
            table_ref[...], jnp.concatenate(hot, axis=1), preferred_element_type=jnp.float32
        ).astype(jnp.bfloat16)

    for g in range(filters):
        rows = slice(g * group, (g + 1) * group)
        lead_rows = slice(channels + g * group, channels + (g + 1) * group)
        tiles = [last[rows, :]] + [feat[rows, b * taps : (b + 1) * taps] for b in range(blocks)]
        window = jnp.concatenate(
            [jnp.concatenate([tiles[b], tiles[b + 1]], axis=1) for b in range(blocks)], axis=0
        )
        conv = jnp.dot(window, toeplitz_ref[g], preferred_element_type=jnp.float32)
        for b in range(blocks):
            cols = slice(b * taps, (b + 1) * taps)
            out_ref[rows, cols] = (
                feat[lead_rows, cols].astype(jnp.float32) * conv[b * group : (b + 1) * group, :]
            ).astype(jnp.bfloat16)
    last[...] = feat[0:channels, (blocks - 1) * taps :]
    rows = send_ref.shape[0]
    total = jnp.dot(weight_ref[2 * rows :, :], out_ref[...], preferred_element_type=jnp.float32)
    pass_ref[...] = total[0:rows]
    send_ref[...] = total[rows:]


def tiles_of(length, taps):
    tile = min(length, 8 * taps)
    assert length % tile == 0
    return tile, length // tile


def column_specs(length, tile, rows):
    if length == tile:
        return [WHOLE for _ in rows]
    return [pl.BlockSpec((count, tile), lambda i: (0, i)) for count in rows]


def hyena(which, group, ids, table, toeplitz, weight, after):
    taps = ids.shape[2]
    channels = table.shape[0] // 2
    vocab = table.shape[1]
    length = ids.shape[0] * taps
    head_dim = weight.shape[0] // 4
    tile, steps = tiles_of(length, taps)
    return pl.pallas_call(
        functools.partial(hyena_kernel, which, group),
        out_shape=[
            jax.ShapeDtypeStruct((channels, length), jnp.bfloat16),
            jax.ShapeDtypeStruct((head_dim, length), jnp.float32),
            jax.ShapeDtypeStruct((head_dim, length), jnp.float32),
        ],
        grid=(steps,),
        in_specs=[WHOLE] * 5,
        out_specs=column_specs(length, tile, (channels, head_dim, head_dim)),
        scratch_shapes=[
            pltpu.VMEM((2 * channels, tile), jnp.bfloat16),
            pltpu.VMEM((channels, taps), jnp.bfloat16),
        ],
        compiler_params=params(),
        cost_estimate=pl.CostEstimate(
            flops=4 * length * channels * (vocab + taps) + 4 * length * channels * head_dim,
            bytes_accessed=8 * 1024 * 1024,
            transcendentals=0,
        ),
    )(ids, table, toeplitz, weight, after)


def project_kernel(mixed_ref, weight_ref, _, own_ref, near_ref):
    rows = own_ref.shape[0]
    total = jnp.dot(
        weight_ref[0 : 2 * rows, :], mixed_ref[...], preferred_element_type=jnp.float32
    )
    own_ref[...] = total[0:rows]
    near_ref[...] = total[rows:]


def project(mixed, weight, taps, after):
    channels, length = mixed.shape
    rows = weight.shape[0] // 4
    tile, steps = tiles_of(length, taps)
    specs = column_specs(length, tile, (channels, rows, rows))
    return pl.pallas_call(
        project_kernel,
        out_shape=[jax.ShapeDtypeStruct((rows, length), jnp.float32)] * 2,
        grid=(steps,),
        in_specs=[specs[0], WHOLE, WHOLE],
        out_specs=specs[1:],
        compiler_params=params(),
        cost_estimate=pl.CostEstimate(
            flops=4 * length * channels * rows, bytes_accessed=1024 * 1024, transcendentals=0
        ),
    )(mixed, weight, after)


def split(exact):
    upper = exact.astype(jnp.bfloat16)
    lower = (exact - upper.astype(jnp.float32)).astype(jnp.bfloat16)
    return jnp.concatenate([upper, lower], axis=0)


def add_kernel(mine_ref, theirs_ref, _, out_ref):
    out_ref[...] = (mine_ref[...] + theirs_ref[...]).astype(out_ref.dtype)


def complete_kernel(own_ref, near_ref, far_ref, mixed_ref):
    mixed_ref[...] = split(own_ref[...] + near_ref[...] + far_ref[...].astype(jnp.float32))


def add_parts(mine, theirs, after):
    return pl.pallas_call(
        add_kernel,
        out_shape=jax.ShapeDtypeStruct(mine.shape, jnp.bfloat16),
        in_specs=[WHOLE] * 3,
        out_specs=WHOLE,
        compiler_params=params(),
        cost_estimate=pl.CostEstimate(
            flops=mine.size, bytes_accessed=10 * mine.size, transcendentals=0
        ),
    )(mine, theirs, after)


def complete(own, near, far):
    rows, length = own.shape
    return pl.pallas_call(
        complete_kernel,
        out_shape=jax.ShapeDtypeStruct((2 * rows, length), jnp.bfloat16),
        in_specs=[WHOLE] * 3,
        out_specs=WHOLE,
        compiler_params=params(),
        cost_estimate=pl.CostEstimate(
            flops=40000 * own.size, bytes_accessed=14 * own.size, transcendentals=0
        ),
    )(own, near, far)


def attend(mixed, w_ref, out_ref):
    head_dim, length = out_ref.shape
    scale = math.log2(math.e) / math.sqrt(head_dim)

    def project_head(which):
        weight = w_ref[which, 0].T
        return jnp.dot(
            jnp.concatenate([weight, weight], axis=1), mixed, preferred_element_type=jnp.float32
        ).astype(jnp.bfloat16)

    queries, keys, values = project_head(0), project_head(1).T, project_head(2)

    def finish(first, parts, values_seen):
        top = functools.reduce(
            jnp.maximum, [jnp.max(part, axis=0, keepdims=True) for part in parts]
        )
        weights = [jnp.exp2((part - top) * scale) for part in parts]
        row_sum = sum(jnp.sum(part, axis=0, keepdims=True) for part in weights)
        probs = jnp.concatenate([part.astype(jnp.bfloat16) for part in weights], axis=0)
        return jnp.dot(values_seen, probs, preferred_element_type=jnp.float32) / row_sum

    def score(keys_seen, queries_block):
        return jnp.dot(keys_seen, queries_block, preferred_element_type=jnp.float32)

    if length <= 2048:
        span = min(512, length)
        row = lax.broadcasted_iota(jnp.int32, (span, span), 0)
        col = lax.broadcasted_iota(jnp.int32, (span, span), 1)
        for first in range(0, length, span):
            cols = slice(first, first + span)
            parts = [jnp.where(row <= col, score(keys[cols], queries[:, cols]), MASKED_SCORE)]
            if first > 0:
                parts = [score(keys[:first], queries[:, cols])] + parts
            out_ref[:, cols] = finish(first, parts, values[:, : first + span])
    else:
        span = 256
        out_ref[...] = queries.astype(jnp.float32)

        @pl.loop(0, length // span)
        def _(i):
            first = pl.multiple_of(i * span, span)
            cols = pl.ds(first, span)
            scores = score(keys, out_ref[:, cols].astype(jnp.bfloat16))
            key_pos = lax.broadcasted_iota(jnp.int32, scores.shape, 0)
            query_pos = first + lax.broadcasted_iota(jnp.int32, scores.shape, 1)
            scores = jnp.where(key_pos <= query_pos, scores, MASKED_SCORE)
            out_ref[:, cols] = finish(first, [scores], values)


def first_kernel(mixed_ref, w_ref, out_ref):
    attend(mixed_ref[...], w_ref, out_ref)


def second_kernel(own_ref, near_ref, far_ref, w_ref, base_ref, ids_ref, out_ref, other):
    exact = own_ref[...] + near_ref[...] + far_ref[...].astype(jnp.float32)
    attend(split(exact), w_ref, other)
    mask = jnp.concatenate(
        [
            ids_ref[b, 2:3, :].astype(jnp.float32) for b in range(ids_ref.shape[0])
        ],
        axis=1,
    )
    difference = (base_ref[...] - other[...]).astype(jnp.bfloat16)
    kept = (difference.astype(jnp.float32) * mask).astype(jnp.bfloat16)
    gram = lax.dot_general(
        kept, difference, (((1,), (1,)), ((), ())), preferred_element_type=jnp.float32
    )
    count = jnp.sum(mask, axis=1, keepdims=True)
    out_ref[...] = gram / jnp.maximum(count, 1.0)


def attention_cost(length, head_dim):
    return pl.CostEstimate(
        flops=4 * length * length * head_dim,
        bytes_accessed=2 * 1024 * 1024,
        transcendentals=length * length // 2,
    )


def attend_first(mixed, w_head):
    head_dim, length = mixed.shape[0] // 2, mixed.shape[1]
    return pl.pallas_call(
        first_kernel,
        out_shape=jax.ShapeDtypeStruct((head_dim, length), jnp.float32),
        in_specs=[WHOLE] * 2,
        out_specs=WHOLE,
        compiler_params=params(),
        cost_estimate=attention_cost(length, head_dim),
    )(mixed, w_head)


def attend_second(own, near, far, w_head, base, ids):
    head_dim, length = own.shape
    return pl.pallas_call(
        second_kernel,
        out_shape=jax.ShapeDtypeStruct((head_dim, head_dim), jnp.float32),
        in_specs=[WHOLE] * 6,
        out_specs=WHOLE,
        scratch_shapes=[pltpu.VMEM((head_dim, length), jnp.float32)],
        compiler_params=params(),
        cost_estimate=attention_cost(length, head_dim),
    )(own, near, far, w_head, base, ids)


def body(token_ids, pair_mask, embed_table, conv_filter, w_out, w_qkv):
    seq_count, mp_count = lax.axis_size("seq"), lax.axis_size("mp")
    channels = embed_table.shape[2]
    filters, taps = conv_filter.shape
    group = channels // filters
    local_heads, head_dim = w_qkv.shape[1], w_qkv.shape[2]
    sharers = seq_count // local_heads
    assert sharers * local_heads == seq_count
    assert mp_count == 4
    assert token_ids.shape[1] % taps == 0

    packed = jnp.concatenate([token_ids, pair_mask[None]], 0)
    table, weight = make_tables(
        (0, 1, 2, 3),
        seq_count,
        local_heads,
        head_dim,
        jnp.transpose(embed_table, (1, 0, 2)),
        w_out,
    )
    (table, weight), conv_filter = lax.optimization_barrier(((table, weight), conv_filter))
    toeplitz = make_toeplitz(conv_filter)
    ids = gather_small(packed, "seq")
    w_head = lax.dynamic_slice_in_dim(w_qkv, head_here(seq_count, local_heads), 1, 1)
    blocks_here = token_ids.shape[1] // taps
    if blocks_here > 1:
        ids = ids.reshape(seq_count, 3, blocks_here, taps).transpose(0, 2, 1, 3)
        ids = ids.reshape(seq_count * blocks_here, 3, taps)

    mixed0, passed0, diagonal0 = hyena(0, group, ids, table, toeplitz, weight, conv_filter)
    diagonal0 = swap(diagonal0, "mp", 1)
    own0, near0 = project(mixed0, weight, taps, conv_filter)
    total0 = add_parts(passed0, diagonal0, own0)
    near0 = swap(near0, "mp", 1)
    far0 = swap(total0, "mp", 2)
    mixed1, passed1, diagonal1 = hyena(1, group, ids, table, toeplitz, weight, total0)
    diagonal1 = swap(diagonal1, "mp", 1)
    complete0 = complete(own0, near0, far0)
    total1 = add_parts(passed1, diagonal1, complete0)
    far1 = swap(total1, "mp", 2)
    own1, near1 = project(mixed1, weight, taps, total1)
    near1 = swap(near1, "mp", 1)
    base = attend_first(complete0, w_head)
    gram = attend_second(own1, near1, far1, w_head, base, ids)
    rows = lax.all_to_all(gram, "seq", 0, 0, tiled=True)
    rows = rows.reshape(local_heads, sharers, head_dim // seq_count, head_dim)
    return rows[:, 0]


def solution(mesh):
    in_specs = (
        P(None, "seq"),
        P("seq"),
        P(None, None, "mp"),
        P("mp", None),
        P("mp", None),
        P(None, "mp", None, None),
    )
    out_specs = P("mp", "seq", None)
    return jax.shard_map(body, mesh=mesh, in_specs=in_specs, out_specs=out_specs, check_vma=False)
```

time: 316 us -> 52.6 us (0.17)
  waiting for transfers between devices: 222 us -> 12.2 us
  matrix products: 42.6 us -> 0 us
  Pallas kernels: 0 us -> 17.1 us
  between operations: 13.9 us -> 0.16 us
  blocking collectives: 19.3 us -> 9.65 us
  other arithmetic: 7.54 us -> 1.5 us
  starting transfers between devices: 5.21 us -> 11.1 us
  local copies, waits for them, and re-layouts: 5.7 us -> 0.64 us
    all_gather x2 -> x0, waiting for transfers between devices: 133 us -> none  [the longest x1 70.7 us: body(): lax.all_gather(key_heads, 'seq', axis=1, tiled=True)]
    reduce_scatter x2 -> x0, waiting for transfers between devices: 87.1 us -> none  [the longest x1 46.8 us: body(): lax.psum_scatter(partial_value, 'mp', scatter_dimension=2, tiled=True)]
    dot_general x9 -> x0, matrix products: 42.6 us -> none  [the longest x1 9.14 us: toeplitz(): jnp.einsum('gj,tsj->gts', conv_filter, selector, preferred_element_type=j...]
    psum x1 -> x0, blocking collectives: 19.3 us -> none  [body(): kept_count = lax.psum(jnp.sum(pair_mask.astype(jnp.float32)), 'seq')]
    pallas_call x0 -> x11, Pallas kernels: none -> 17.1 us  [the longest x2 8.17 us: hyena(): pl.pallas_call(functools.partial(hyena_kernel, which, group), out_shape=[...]
    ppermute x1 -> x10, waiting for transfers between devices: 1.88 us -> 12.2 us  [swap(): return lax.ppermute(value, axis, [(i, i ^ turn) for i in range(count)])]
    all_to_all x0 -> x1, blocking collectives: none -> 9.65 us  [body(): rows = lax.all_to_all(gram, 'seq', 0, 0, tiled=True)]
    ppermute x1 -> x10, starting transfers between devices: 4.9 us -> 11.1 us  [swap(): return lax.ppermute(value, axis, [(i, i ^ turn) for i in range(count)])]
  transfers between devices with their start and end apart: 5 -> 10, of which waited for: 5 -> 6; matrix products, arithmetic and copies ran while one was open for 8% -> 0% of each run, Pallas kernels for 0% -> 20%
where the time goes in v1:
time: 52.6 us; the launch traced here: 52.4 us
  Pallas kernels  17.1 us (33%)
  waiting for transfers between devices  12.2 us (23%)
  starting transfers between devices  11.1 us (21%)
  blocking collectives  9.65 us (18%)
  other arithmetic  1.5 us (3%)
  local copies, waits for them, and re-layouts  0.64 us (1%)
    ppermute x10, waiting for transfers between devices, swap(): return lax.ppermute(value, axis, [(i, i ^ turn) for i in range(count)])  12.2 us
    ppermute x10, starting transfers between devices, swap(): return lax.ppermute(value, axis, [(i, i ^ turn) for i in range(count)])  11.1 us
    all_to_all x1, blocking collectives, body(): rows = lax.all_to_all(gram, 'seq', 0, 0, tiled=True)  9.65 us
    pallas_call x2, Pallas kernels, hyena(): pl.pallas_call(functools.partial(hyena_kernel, which, group), out_shape=[...  8.17 us
    pallas_call x1, Pallas kernels, make_tables(): pl.pallas_call(functools.partial(tables_kernel, order, local_heads, seq_c...  3.14 us
    pallas_call x1, Pallas kernels, attend_second(): pl.pallas_call(second_kernel, out_shape=jax.ShapeDtypeStruct((head_dim, h...  1.83 us
    pallas_call x1, Pallas kernels, attend_first(): pl.pallas_call(first_kernel, out_shape=jax.ShapeDtypeStruct((head_dim, le...  1.63 us
    pallas_call x2, Pallas kernels, project(): pl.pallas_call(project_kernel, out_shape=[jax.ShapeDtypeStruct((rows, len...  1.41 us
  transfers between devices with their start and end apart: 10, of which 6 were waited for; matrix products, arithmetic and copies ran while one was open for 0% of the time, Pallas kernels for 20%

profile of v1, /device:TPU:0, one launch (start us, length us, event | category | flops | bytes accessed | tf_op | source)
XLA Modules:
  0.0 52.4 jit_solution(9717255700508512830)
XLA Ops:
  0.0 0.0 copy-start
  0.0 0.8 %add_bitcast_fusion = s32[1,3,128]{2,1,0:T(4,128)S(1)} fusion(s32[1,128]{1,0:T(1,128)} %bitcast.15, s32[2,128]{1,0:T(2,128)} %param.6), kind=kLoop, calls=%fused_computation.4 | loop fusion | flops 384 | bytes 3072 | tf_op jit(solution)/shard_map/broadcast_in_dim | solution.py:35
  0.8 4.0 %collective-permute-start = (s32[1,3,128]{2,1,0:T(4,128)S(1)}, s32[1,3,128]{2,1,0:T(4,128)S(1)}, u32[]{:S(2)}, u32[]{:S(2)}) collective-permute-start(s32[1,3,128]{2,1,0:T(4,128)S(1)} %add_bitcast_fusion), channel_id=1, source_target_pairs={{0,12},{4,8},{8,4},{12,0},{16,28},{20,24},{24,20},{28,16},{1,13},{... | collective-permute-start | bytes 4616 | tf_op jit(solution)/shard_map/ppermute | solution.py:30
  4.8 0.4 collective-permute-start.1
  5.2 0.2 collective-permute-start.2
  5.4 0.9 %collective-permute-done = s32[1,3,128]{2,1,0:T(4,128)S(1)} collective-permute-done((s32[1,3,128]{2,1,0:T(4,128)S(1)}, s32[1,3,128]{2,1,0:T(4,128)S(1)}, u32[]{:S(2)}, u32[]{:S(2)}) %collective-permute-start) | collective-permute-done | bytes 1568 | tf_op jit(solution)/shard_map/ppermute | solution.py:30
  6.3 2.0 %collective-permute-done.1 = s32[1,3,128]{2,1,0:T(4,128)S(1)} collective-permute-done((s32[1,3,128]{2,1,0:T(4,128)S(1)}, s32[1,3,128]{2,1,0:T(4,128)S(1)}, u32[]{:S(2)}, u32[]{:S(2)}) %collective-permute-start.1) | collective-permute-done | bytes 1568 | tf_op jit(solution)/shard_map/ppermute | solution.py:30
  8.3 0.4 collective-permute-done.2
  8.8 0.7 %broadcast_select_fusion.9 = (s32[1,3,128]{2,1,0:T(4,128)S(1)}, s32[1,3,128]{2,1,0:T(4,128)S(1)}, s32[1,3,128]{2,1,0:T(4,128)S(1)}, s32[1,3,128]{2,1,0:T(4,128)S(1)}) fusion(pred[]{:T(512)S(6)} %eq.10, s32[1,3,128]{2,1,0:T(4,128)S(1)} %collective-permute-done, s32[1,3,128]{2,1,0:T(4,128)S(1)} %collective-permute-done.1, pred[]{:T(512)S(6)} %eq.11, ...), kind=kLoop, calls=%fused_computation.12 | loop fusion | flops 3456 | bytes 12290 | tf_op jit(solution)/shard_map/jit(_where)/select_n | solution.py:45
  9.5 2.7 %collective-permute-start.3 = (s32[4,3,128]{2,1,0:T(4,128)S(1)}, s32[4,3,128]{2,1,0:T(4,128)S(1)}, u32[]{:S(2)}, u32[]{:S(2)}) collective-permute-start(s32[4,3,128]{2,1,0:T(4,128)S(1)} %pad_add_fusion.1), channel_id=1, source_target_pairs={{0,16},{4,20},{8,24},{12,28},{16,0},{20,4},{24,8},{28,12},{1,17},{... | collective-permute-start | bytes 18440 | tf_op jit(solution)/shard_map/ppermute | solution.py:30
  12.2 0.0 copy-start.1
  12.2 3.1 %shard_map.64 = (bf16[2048,512]{1,0:T(8,128)(2,1)S(1)}, bf16[512,1024]{1,0:T(8,128)(2,1)S(1)}) custom-call(bf16[3,512,1024]{2,1,0:T(8,128)(2,1)} %bitcast.14, bf16[1024,4096]{1,0:T(8,128)(2,1)} %w_out_ref.1), custom_call_target="tpu_custom_call" | custom-call | flops 2097152 | bytes 8388608 | tf_op jit(solution)/shard_map/pallas_call | solution.py:102
  15.3 0.0 copy-done.1
  15.3 0.7 %shard_map.65.toeplitz_ref = bf16[64,256,128]{2,1,0:T(8,128)(2,1)S(1)} custom-call(bf16[64,128]{1,0:T(8,128)(2,1)S(1)} %copy-done.1), custom_call_target="tpu_custom_call" | custom-call | flops 4194304 | bytes 4194304 | tf_op jit(solution)/shard_map/pallas_call | solution.py:138
  16.0 0.0 collective-permute-done.3
  16.1 4.1 %shard_map.66 = (bf16[1024,1024]{1,0:T(8,128)(2,1)S(1)}, f32[128,1024]{1,0:T(8,128)S(1)}, f32[128,1024]{1,0:T(8,128)S(1)}) custom-call(s32[8,3,128]{2,1,0:T(4,128)S(1)} %pad_add_fusion.ids_ref, bf16[2048,512]{1,0:T(8,128)(2,1)S(1)} %get-tuple-element.22.table_ref, bf16[64,256,128]{2,1,0:T(8,128)(2,1)S(1)} %shard_map.65.toeplitz_ref, ...), custom_call_target="tpu_custom_call" | custom-call | flops 3221225472 | bytes 8388608 | tf_op jit(solution)/shard_map/pallas_call | solution.py:228
  20.2 0.1 collective-permute-start.4
  20.2 0.7 %shard_map.67 = (f32[128,1024]{1,0:T(8,128)S(1)}, f32[128,1024]{1,0:T(8,128)S(1)}) custom-call(bf16[1024,1024]{1,0:T(8,128)(2,1)S(1)} %get-tuple-element.27.mixed_ref, bf16[512,1024]{1,0:T(8,128)(2,1)S(1)} %get-tuple-element.24.weight_ref, bf16[64,128]{1,0:T(8,128)(2,1)S(1)} %copy-done.1), custom_call_target="tpu_custom_call" | custom-call | flops 536870912 | bytes 1048576 | tf_op jit(solution)/shard_map/pallas_call | solution.py:265
  21.0 0.6 %collective-permute-start.6 = (f32[128,1024]{1,0:T(8,128)S(1)}, f32[128,1024]{1,0:T(8,128)S(1)}, u32[]{:S(2)}, u32[]{:S(2)}) collective-permute-start(f32[128,1024]{1,0:T(8,128)S(1)} %get-tuple-element.32), channel_id=1, source_target_pairs={{0,1},{1,0},{2,3},{3,2},{4,5},{5,4},{6,7},{7,6},{8,9},{9,8},{10,11... | collective-permute-start | bytes 1572872 | tf_op jit(solution)/shard_map/ppermute | solution.py:30
  21.5 0.6 %collective-permute-done.4.theirs_ref = f32[128,1024]{1,0:T(8,128)S(1)} collective-permute-done((f32[128,1024]{1,0:T(8,128)S(1)}, f32[128,1024]{1,0:T(8,128)S(1)}, u32[]{:S(2)}, u32[]{:S(2)}) %collective-permute-start.4) | collective-permute-done | bytes 524320 | tf_op jit(solution)/shard_map/ppermute | solution.py:30
  22.2 1.6 %collective-permute-start.7 = (bf16[128,1024]{1,0:T(8,128)(2,1)S(1)}, bf16[128,1024]{1,0:T(8,128)(2,1)S(1)}, u32[]{:S(2)}, u32[]{:S(2)}) collective-permute-start(bf16[128,1024]{1,0:T(8,128)(2,1)S(1)} %shard_map.68._), channel_id=1, source_target_pairs={{0,2},{1,3},{2,0},{3,1},{4,6},{5,7},{6,4},{7,5},{8,10},{9,11},{10,... | collective-permute-start | bytes 786440 | tf_op jit(solution)/shard_map/ppermute | solution.py:30
  23.7 4.1 %shard_map.69 = (bf16[1024,1024]{1,0:T(8,128)(2,1)S(1)}, f32[128,1024]{1,0:T(8,128)S(1)}, f32[128,1024]{1,0:T(8,128)S(1)}) custom-call(s32[8,3,128]{2,1,0:T(4,128)S(1)} %pad_add_fusion.ids_ref, bf16[2048,512]{1,0:T(8,128)(2,1)S(1)} %get-tuple-element.22.table_ref, bf16[64,256,128]{2,1,0:T(8,128)(2,1)S(1)} %shard_map.65.toeplitz_ref, ...), custom_call_target="tpu_custom_call" | custom-call | flops 3221225472 | bytes 8388608 | tf_op jit(solution)/shard_map/pallas_call | solution.py:228
  27.8 0.1 collective-permute-start.5
  27.9 0.0 collective-permute-done.6.near_ref
  27.9 2.7 %collective-permute-done.7.far_ref = bf16[128,1024]{1,0:T(8,128)(2,1)S(1)} collective-permute-done((bf16[128,1024]{1,0:T(8,128)(2,1)S(1)}, bf16[128,1024]{1,0:T(8,128)(2,1)S(1)}, u32[]{:S(2)}, u32[]{:S(2)}) %collective-permute-start.7) | collective-permute-done | bytes 262176 | tf_op jit(solution)/shard_map/ppermute | solution.py:30
  30.6 0.1 shard_map.70._.mixed_ref
  30.7 0.0 collective-permute-done.5.theirs_ref
  30.7 0.1 shard_map.71._
  30.8 0.7 %shard_map.72 = (f32[128,1024]{1,0:T(8,128)S(1)}, f32[128,1024]{1,0:T(8,128)S(1)}) custom-call(bf16[1024,1024]{1,0:T(8,128)(2,1)S(1)} %get-tuple-element.29.mixed_ref, bf16[512,1024]{1,0:T(8,128)(2,1)S(1)} %get-tuple-element.24.weight_ref, bf16[128,1024]{1,0:T(8,128)(2,1)S(1)} %shard_map.71._), custom_call_target="tpu_custom_call" | custom-call | flops 536870912 | bytes 1048576 | tf_op jit(solution)/shard_map/pallas_call | solution.py:265
  31.5 0.1 collective-permute-start.8
  31.6 1.6 %collective-permute-start.9 = (bf16[128,1024]{1,0:T(8,128)(2,1)S(1)}, bf16[128,1024]{1,0:T(8,128)(2,1)S(1)}, u32[]{:S(2)}, u32[]{:S(2)}) collective-permute-start(bf16[128,1024]{1,0:T(8,128)(2,1)S(1)} %shard_map.71._), channel_id=1, source_target_pairs={{0,2},{1,3},{2,0},{3,1},{4,6},{5,7},{6,4},{7,5},{8,10},{9,11},{10,... | collective-permute-start | bytes 786440 | tf_op jit(solution)/shard_map/ppermute | solution.py:30
  33.1 0.0 copy-done
  33.2 1.6 %shard_map.73.base_ref = f32[128,1024]{1,0:T(8,128)S(1)} custom-call(bf16[256,1024]{1,0:T(8,128)(2,1)S(1)} %shard_map.70._.mixed_ref, bf16[3,1,128,128]{3,2,1,0:T(8,128)(2,1)S(1)} %constant_dynamic-slice_fusion.w_ref), custom_call_target="tpu_custom_call" | custom-call | flops 536870912 | bytes 2097152 | tf_op jit(solution)/shard_map/pallas_call | solution.py:400
  34.8 5.5 %collective-permute-done.9.far_ref = bf16[128,1024]{1,0:T(8,128)(2,1)S(1)} collective-permute-done((bf16[128,1024]{1,0:T(8,128)(2,1)S(1)}, bf16[128,1024]{1,0:T(8,128)(2,1)S(1)}, u32[]{:S(2)}, u32[]{:S(2)}) %collective-permute-start.9) | collective-permute-done | bytes 262176 | tf_op jit(solution)/shard_map/ppermute | solution.py:30
  40.3 0.0 collective-permute-done.8.near_ref
  40.3 1.8 %shard_map.74 = f32[128,128]{1,0:T(8,128)S(1)} custom-call(f32[128,1024]{1,0:T(8,128)S(1)} %get-tuple-element.33.own_ref, f32[128,1024]{1,0:T(8,128)S(1)} %collective-permute-done.8.near_ref, bf16[128,1024]{1,0:T(8,128)(2,1)S(1)} %collective-permute-done.9.far_ref, bf16[3,1,128,128]{3,2,1,0:T(8,128)(2,1)S(1)} %constant_dynamic-slice_fusion.w_ref, ...), custom_call_target="tpu_custom_call" | custom-call | flops 536870912 | bytes 2097152 | tf_op jit(solution)/shard_map/pallas_call | solution.py:412
  42.1 9.7 %all_to_all.9 = f32[8,16,128]{2,1,0:T(8,128)S(1)} all-to-all(f32[8,16,128]{2,1,0:T(8,128)S(1)} %bitcast.13), channel_id=1, replica_groups=mesh['seq'=8,'mp'=4] {'seq'}, dimensions={0} | all-to-all | bytes 131072 | tf_op jit(solution)/shard_map/all_to_all | solution.py:467
  51.8 0.6 %copy.8 = f32[8,16,128]{2,1,0:T(8,128)} copy(f32[8,16,128]{2,1,0:T(8,128)S(1)} %all_to_all.9) | data formatting | bytes 131072
  (5 shorter events, 0.1 us)
Async XLA Ops:
  0.0 33.1 %copy-start = (bf16[3,8,128,128]{3,2,1,0:T(8,128)(2,1)S(1)}, bf16[3,8,128,128]{3,2,1,0:T(8,128)(2,1)}, u32[]{:S(2)}) copy-start(bf16[3,8,128,128]{3,2,1,0:T(8,128)(2,1)} %param.11) | copy-start | bytes 2359300
  0.8 5.5 %collective-permute-start = (s32[1,3,128]{2,1,0:T(4,128)S(1)}, s32[1,3,128]{2,1,0:T(4,128)S(1)}, u32[]{:S(2)}, u32[]{:S(2)}) collective-permute-start(s32[1,3,128]{2,1,0:T(4,128)S(1)} %add_bitcast_fusion), channel_id=1, source_target_pairs={{0,12},{4,8},{8,4},{12,0},{16,28},{20,24},{24,20},{28,16},{1,13},{... | collective-permute-start | bytes 4616 | tf_op jit(solution)/shard_map/ppermute | solution.py:30
  4.8 3.6 %collective-permute-start.1 = (s32[1,3,128]{2,1,0:T(4,128)S(1)}, s32[1,3,128]{2,1,0:T(4,128)S(1)}, u32[]{:S(2)}, u32[]{:S(2)}) collective-permute-start(s32[1,3,128]{2,1,0:T(4,128)S(1)} %add_bitcast_fusion), channel_id=1, source_target_pairs={{0,8},{4,12},{8,0},{12,4},{16,24},{20,28},{24,16},{28,20},{1,9},{5... | collective-permute-start | bytes 4616 | tf_op jit(solution)/shard_map/ppermute | solution.py:30
  5.2 3.6 %collective-permute-start.2 = (s32[1,3,128]{2,1,0:T(4,128)S(1)}, s32[1,3,128]{2,1,0:T(4,128)S(1)}, u32[]{:S(2)}, u32[]{:S(2)}) collective-permute-start(s32[1,3,128]{2,1,0:T(4,128)S(1)} %add_bitcast_fusion), channel_id=1, source_target_pairs={{0,4},{4,0},{8,12},{12,8},{16,20},{20,16},{24,28},{28,24},{1,5},{5... | collective-permute-start | bytes 4616 | tf_op jit(solution)/shard_map/ppermute | solution.py:30
  9.5 6.5 %collective-permute-start.3 = (s32[4,3,128]{2,1,0:T(4,128)S(1)}, s32[4,3,128]{2,1,0:T(4,128)S(1)}, u32[]{:S(2)}, u32[]{:S(2)}) collective-permute-start(s32[4,3,128]{2,1,0:T(4,128)S(1)} %pad_add_fusion.1), channel_id=1, source_target_pairs={{0,16},{4,20},{8,24},{12,28},{16,0},{20,4},{24,8},{28,12},{1,17},{... | collective-permute-start | bytes 18440 | tf_op jit(solution)/shard_map/ppermute | solution.py:30
  12.2 3.1 %copy-start.1 = (bf16[64,128]{1,0:T(8,128)(2,1)S(1)}, bf16[64,128]{1,0:T(8,128)(2,1)}, u32[]{:S(2)}) copy-start(bf16[64,128]{1,0:T(8,128)(2,1)} %_.1) | copy-start | bytes 49156
  20.2 2.0 %collective-permute-start.4 = (f32[128,1024]{1,0:T(8,128)S(1)}, f32[128,1024]{1,0:T(8,128)S(1)}, u32[]{:S(2)}, u32[]{:S(2)}) collective-permute-start(f32[128,1024]{1,0:T(8,128)S(1)} %get-tuple-element.26), channel_id=1, source_target_pairs={{0,1},{1,0},{2,3},{3,2},{4,5},{5,4},{6,7},{7,6},{8,9},{9,8},{10,11... | collective-permute-start | bytes 1572872 | tf_op jit(solution)/shard_map/ppermute | solution.py:30
  21.0 7.0 %collective-permute-start.6 = (f32[128,1024]{1,0:T(8,128)S(1)}, f32[128,1024]{1,0:T(8,128)S(1)}, u32[]{:S(2)}, u32[]{:S(2)}) collective-permute-start(f32[128,1024]{1,0:T(8,128)S(1)} %get-tuple-element.32), channel_id=1, source_target_pairs={{0,1},{1,0},{2,3},{3,2},{4,5},{5,4},{6,7},{7,6},{8,9},{9,8},{10,11... | collective-permute-start | bytes 1572872 | tf_op jit(solution)/shard_map/ppermute | solution.py:30
  22.2 8.4 %collective-permute-start.7 = (bf16[128,1024]{1,0:T(8,128)(2,1)S(1)}, bf16[128,1024]{1,0:T(8,128)(2,1)S(1)}, u32[]{:S(2)}, u32[]{:S(2)}) collective-permute-start(bf16[128,1024]{1,0:T(8,128)(2,1)S(1)} %shard_map.68._), channel_id=1, source_target_pairs={{0,2},{1,3},{2,0},{3,1},{4,6},{5,7},{6,4},{7,5},{8,10},{9,11},{10,... | collective-permute-start | bytes 786440 | tf_op jit(solution)/shard_map/ppermute | solution.py:30
  27.8 2.9 %collective-permute-start.5 = (f32[128,1024]{1,0:T(8,128)S(1)}, f32[128,1024]{1,0:T(8,128)S(1)}, u32[]{:S(2)}, u32[]{:S(2)}) collective-permute-start(f32[128,1024]{1,0:T(8,128)S(1)} %get-tuple-element.31), channel_id=1, source_target_pairs={{0,1},{1,0},{2,3},{3,2},{4,5},{5,4},{6,7},{7,6},{8,9},{9,8},{10,11... | collective-permute-start | bytes 1572872 | tf_op jit(solution)/shard_map/ppermute | solution.py:30
  31.5 8.8 %collective-permute-start.8 = (f32[128,1024]{1,0:T(8,128)S(1)}, f32[128,1024]{1,0:T(8,128)S(1)}, u32[]{:S(2)}, u32[]{:S(2)}) collective-permute-start(f32[128,1024]{1,0:T(8,128)S(1)} %get-tuple-element.34), channel_id=1, source_target_pairs={{0,1},{1,0},{2,3},{3,2},{4,5},{5,4},{6,7},{7,6},{8,9},{9,8},{10,11... | collective-permute-start | bytes 1572872 | tf_op jit(solution)/shard_map/ppermute | solution.py:30
  31.6 8.7 %collective-permute-start.9 = (bf16[128,1024]{1,0:T(8,128)(2,1)S(1)}, bf16[128,1024]{1,0:T(8,128)(2,1)S(1)}, u32[]{:S(2)}, u32[]{:S(2)}) collective-permute-start(bf16[128,1024]{1,0:T(8,128)(2,1)S(1)} %shard_map.71._), channel_id=1, source_target_pairs={{0,2},{1,3},{2,0},{3,1},{4,6},{5,7},{6,4},{7,5},{8,10},{9,11},{10,... | collective-permute-start | bytes 786440 | tf_op jit(solution)/shard_map/ppermute | solution.py:30

commit v2 on v1

--- a/solution.py
+++ b/solution.py
@@ -281,7 +281,8 @@
     return jnp.concatenate([upper, lower], axis=0)
 
 
-def add_kernel(mine_ref, theirs_ref, _, out_ref):
+def add_kernel(mine_ref, theirs_ref, *refs):
+    out_ref = refs[-1]
     out_ref[...] = (mine_ref[...] + theirs_ref[...]).astype(out_ref.dtype)
 
 
@@ -293,13 +294,13 @@
     return pl.pallas_call(
         add_kernel,
         out_shape=jax.ShapeDtypeStruct(mine.shape, jnp.bfloat16),
-        in_specs=[WHOLE] * 3,
+        in_specs=[WHOLE] * (2 + len(after)),
         out_specs=WHOLE,
         compiler_params=params(),
         cost_estimate=pl.CostEstimate(
             flops=mine.size, bytes_accessed=10 * mine.size, transcendentals=0
         ),
-    )(mine, theirs, after)
+    )(mine, theirs, *after)
 
 
 def complete(own, near, far):
@@ -452,16 +453,16 @@
     mixed0, passed0, diagonal0 = hyena(0, group, ids, table, toeplitz, weight, conv_filter)
     diagonal0 = swap(diagonal0, "mp", 1)
     own0, near0 = project(mixed0, weight, taps, conv_filter)
-    total0 = add_parts(passed0, diagonal0, own0)
+    total0 = add_parts(passed0, diagonal0, [own0])
     near0 = swap(near0, "mp", 1)
     far0 = swap(total0, "mp", 2)
     mixed1, passed1, diagonal1 = hyena(1, group, ids, table, toeplitz, weight, total0)
     diagonal1 = swap(diagonal1, "mp", 1)
+    own1, near1 = project(mixed1, weight, taps, conv_filter)
     complete0 = complete(own0, near0, far0)
-    total1 = add_parts(passed1, diagonal1, complete0)
+    total1 = add_parts(passed1, diagonal1, [complete0, own1])
+    near1 = swap(near1, "mp", 1)
     far1 = swap(total1, "mp", 2)
-    own1, near1 = project(mixed1, weight, taps, total1)
-    near1 = swap(near1, "mp", 1)
     base = attend_first(complete0, w_head)
     gram = attend_second(own1, near1, far1, w_head, base, ids)
     rows = lax.all_to_all(gram, "seq", 0, 0, tiled=True)

time: 52.6 us -> 50.7 us (0.964)
  waiting for transfers between devices: 12.2 us -> 9.83 us
    ppermute x10, waiting for transfers between devices: 12.2 us -> 9.83 us  [swap(): return lax.ppermute(value, axis, [(i, i ^ turn) for i in range(count)])]
  transfers between devices with their start and end apart: 10 -> 10, of which waited for: 6 -> 6; matrix products, arithmetic and copies ran while one was open for 0% -> 0% of each run, Pallas kernels for 20% -> 22%
where the time goes in v2:
time: 50.7 us; the launch traced here: 50.5 us
  Pallas kernels  17.1 us (34%)
  starting transfers between devices  11.6 us (23%)
  waiting for transfers between devices  9.83 us (19%)
  blocking collectives  9.64 us (19%)
  other arithmetic  1.5 us (3%)
  local copies, waits for them, and re-layouts  0.64 us (1%)
    ppermute x10, starting transfers between devices, swap(): return lax.ppermute(value, axis, [(i, i ^ turn) for i in range(count)])  11.6 us
    ppermute x10, waiting for transfers between devices, swap(): return lax.ppermute(value, axis, [(i, i ^ turn) for i in range(count)])  9.83 us
    all_to_all x1, blocking collectives, body(): rows = lax.all_to_all(gram, 'seq', 0, 0, tiled=True)  9.64 us
    pallas_call x2, Pallas kernels, hyena(): pl.pallas_call(functools.partial(hyena_kernel, which, group), out_shape=[...  8.17 us
    pallas_call x1, Pallas kernels, make_tables(): pl.pallas_call(functools.partial(tables_kernel, order, local_heads, seq_c...  3.14 us
    pallas_call x1, Pallas kernels, attend_second(): pl.pallas_call(second_kernel, out_shape=jax.ShapeDtypeStruct((head_dim, h...  1.83 us
    pallas_call x1, Pallas kernels, attend_first(): pl.pallas_call(first_kernel, out_shape=jax.ShapeDtypeStruct((head_dim, le...  1.63 us
    pallas_call x2, Pallas kernels, project(): pl.pallas_call(project_kernel, out_shape=[jax.ShapeDtypeStruct((rows, len...  1.41 us
  transfers between devices with their start and end apart: 10, of which 6 were waited for; matrix products, arithmetic and copies ran while one was open for 0% of the time, Pallas kernels for 22%

profile of v2, /device:TPU:0, one launch (start us, length us, event | category | flops | bytes accessed | tf_op | source)
XLA Modules:
  0.0 50.5 jit_solution(5152201883320773471)
XLA Ops:
  0.0 0.0 copy-start
  0.0 0.8 %add_bitcast_fusion = s32[1,3,128]{2,1,0:T(4,128)S(1)} fusion(s32[1,128]{1,0:T(1,128)} %bitcast.15, s32[2,128]{1,0:T(2,128)} %param.6), kind=kLoop, calls=%fused_computation.4 | loop fusion | flops 384 | bytes 3072 | tf_op jit(solution)/shard_map/broadcast_in_dim | solution.py:35
  0.8 4.0 %collective-permute-start = (s32[1,3,128]{2,1,0:T(4,128)S(1)}, s32[1,3,128]{2,1,0:T(4,128)S(1)}, u32[]{:S(2)}, u32[]{:S(2)}) collective-permute-start(s32[1,3,128]{2,1,0:T(4,128)S(1)} %add_bitcast_fusion), channel_id=1, source_target_pairs={{0,12},{4,8},{8,4},{12,0},{16,28},{20,24},{24,20},{28,16},{1,13},{... | collective-permute-start | bytes 4616 | tf_op jit(solution)/shard_map/ppermute | solution.py:30
  4.8 0.4 collective-permute-start.1
  5.2 0.2 collective-permute-start.2
  5.4 0.9 %collective-permute-done = s32[1,3,128]{2,1,0:T(4,128)S(1)} collective-permute-done((s32[1,3,128]{2,1,0:T(4,128)S(1)}, s32[1,3,128]{2,1,0:T(4,128)S(1)}, u32[]{:S(2)}, u32[]{:S(2)}) %collective-permute-start) | collective-permute-done | bytes 1568 | tf_op jit(solution)/shard_map/ppermute | solution.py:30
  6.3 2.0 %collective-permute-done.1 = s32[1,3,128]{2,1,0:T(4,128)S(1)} collective-permute-done((s32[1,3,128]{2,1,0:T(4,128)S(1)}, s32[1,3,128]{2,1,0:T(4,128)S(1)}, u32[]{:S(2)}, u32[]{:S(2)}) %collective-permute-start.1) | collective-permute-done | bytes 1568 | tf_op jit(solution)/shard_map/ppermute | solution.py:30
  8.3 0.4 collective-permute-done.2
  8.8 0.7 %broadcast_select_fusion.9 = (s32[1,3,128]{2,1,0:T(4,128)S(1)}, s32[1,3,128]{2,1,0:T(4,128)S(1)}, s32[1,3,128]{2,1,0:T(4,128)S(1)}, s32[1,3,128]{2,1,0:T(4,128)S(1)}) fusion(pred[]{:T(512)S(6)} %eq.10, s32[1,3,128]{2,1,0:T(4,128)S(1)} %collective-permute-done, s32[1,3,128]{2,1,0:T(4,128)S(1)} %collective-permute-done.1, pred[]{:T(512)S(6)} %eq.11, ...), kind=kLoop, calls=%fused_computation.12 | loop fusion | flops 3456 | bytes 12290 | tf_op jit(solution)/shard_map/jit(_where)/select_n | solution.py:45
  9.5 2.7 %collective-permute-start.3 = (s32[4,3,128]{2,1,0:T(4,128)S(1)}, s32[4,3,128]{2,1,0:T(4,128)S(1)}, u32[]{:S(2)}, u32[]{:S(2)}) collective-permute-start(s32[4,3,128]{2,1,0:T(4,128)S(1)} %pad_add_fusion.1), channel_id=1, source_target_pairs={{0,16},{4,20},{8,24},{12,28},{16,0},{20,4},{24,8},{28,12},{1,17},{... | collective-permute-start | bytes 18440 | tf_op jit(solution)/shard_map/ppermute | solution.py:30
  12.2 0.0 copy-start.1
  12.2 3.1 %shard_map.64 = (bf16[2048,512]{1,0:T(8,128)(2,1)S(1)}, bf16[512,1024]{1,0:T(8,128)(2,1)S(1)}) custom-call(bf16[3,512,1024]{2,1,0:T(8,128)(2,1)} %bitcast.14, bf16[1024,4096]{1,0:T(8,128)(2,1)} %w_out_ref.1), custom_call_target="tpu_custom_call" | custom-call | flops 2097152 | bytes 8388608 | tf_op jit(solution)/shard_map/pallas_call | solution.py:102
  15.3 0.0 copy-done.1
  15.3 0.7 %shard_map.65.toeplitz_ref = bf16[64,256,128]{2,1,0:T(8,128)(2,1)S(1)} custom-call(bf16[64,128]{1,0:T(8,128)(2,1)S(1)} %copy-done.1), custom_call_target="tpu_custom_call" | custom-call | flops 4194304 | bytes 4194304 | tf_op jit(solution)/shard_map/pallas_call | solution.py:138
  16.0 0.0 collective-permute-done.3
  16.1 4.1 %shard_map.66 = (bf16[1024,1024]{1,0:T(8,128)(2,1)S(1)}, f32[128,1024]{1,0:T(8,128)S(1)}, f32[128,1024]{1,0:T(8,128)S(1)}) custom-call(s32[8,3,128]{2,1,0:T(4,128)S(1)} %pad_add_fusion.ids_ref, bf16[2048,512]{1,0:T(8,128)(2,1)S(1)} %get-tuple-element.22.table_ref, bf16[64,256,128]{2,1,0:T(8,128)(2,1)S(1)} %shard_map.65.toeplitz_ref, ...), custom_call_target="tpu_custom_call" | custom-call | flops 3221225472 | bytes 8388608 | tf_op jit(solution)/shard_map/pallas_call | solution.py:228
  20.2 0.1 collective-permute-start.4
  20.2 0.7 %shard_map.67 = (f32[128,1024]{1,0:T(8,128)S(1)}, f32[128,1024]{1,0:T(8,128)S(1)}) custom-call(bf16[1024,1024]{1,0:T(8,128)(2,1)S(1)} %get-tuple-element.27.mixed_ref, bf16[512,1024]{1,0:T(8,128)(2,1)S(1)} %get-tuple-element.24.weight_ref, bf16[64,128]{1,0:T(8,128)(2,1)S(1)} %copy-done.1), custom_call_target="tpu_custom_call" | custom-call | flops 536870912 | bytes 1048576 | tf_op jit(solution)/shard_map/pallas_call | solution.py:265
  21.0 0.6 %collective-permute-start.7 = (f32[128,1024]{1,0:T(8,128)S(1)}, f32[128,1024]{1,0:T(8,128)S(1)}, u32[]{:S(2)}, u32[]{:S(2)}) collective-permute-start(f32[128,1024]{1,0:T(8,128)S(1)} %get-tuple-element.34), channel_id=1, source_target_pairs={{0,1},{1,0},{2,3},{3,2},{4,5},{5,4},{6,7},{7,6},{8,9},{9,8},{10,11... | collective-permute-start | bytes 1572872 | tf_op jit(solution)/shard_map/ppermute | solution.py:30
  21.5 0.6 %collective-permute-done.4.theirs_ref = f32[128,1024]{1,0:T(8,128)S(1)} collective-permute-done((f32[128,1024]{1,0:T(8,128)S(1)}, f32[128,1024]{1,0:T(8,128)S(1)}, u32[]{:S(2)}, u32[]{:S(2)}) %collective-permute-start.4) | collective-permute-done | bytes 524320 | tf_op jit(solution)/shard_map/ppermute | solution.py:30
  22.2 1.6 %collective-permute-start.8 = (bf16[128,1024]{1,0:T(8,128)(2,1)S(1)}, bf16[128,1024]{1,0:T(8,128)(2,1)S(1)}, u32[]{:S(2)}, u32[]{:S(2)}) collective-permute-start(bf16[128,1024]{1,0:T(8,128)(2,1)S(1)} %shard_map.68._), channel_id=1, source_target_pairs={{0,2},{1,3},{2,0},{3,1},{4,6},{5,7},{6,4},{7,5},{8,10},{9,11},{10,... | collective-permute-start | bytes 786440 | tf_op jit(solution)/shard_map/ppermute | solution.py:30
  23.7 4.1 %shard_map.69 = (bf16[1024,1024]{1,0:T(8,128)(2,1)S(1)}, f32[128,1024]{1,0:T(8,128)S(1)}, f32[128,1024]{1,0:T(8,128)S(1)}) custom-call(s32[8,3,128]{2,1,0:T(4,128)S(1)} %pad_add_fusion.ids_ref, bf16[2048,512]{1,0:T(8,128)(2,1)S(1)} %get-tuple-element.22.table_ref, bf16[64,256,128]{2,1,0:T(8,128)(2,1)S(1)} %shard_map.65.toeplitz_ref, ...), custom_call_target="tpu_custom_call" | custom-call | flops 3221225472 | bytes 8388608 | tf_op jit(solution)/shard_map/pallas_call | solution.py:228
  27.8 0.1 collective-permute-start.6
  27.9 0.7 %shard_map.70 = (f32[128,1024]{1,0:T(8,128)S(1)}, f32[128,1024]{1,0:T(8,128)S(1)}) custom-call(bf16[1024,1024]{1,0:T(8,128)(2,1)S(1)} %get-tuple-element.29.mixed_ref, bf16[512,1024]{1,0:T(8,128)(2,1)S(1)} %get-tuple-element.24.weight_ref, bf16[64,128]{1,0:T(8,128)(2,1)S(1)} %copy-done.1), custom_call_target="tpu_custom_call" | custom-call | flops 536870912 | bytes 1048576 | tf_op jit(solution)/shard_map/pallas_call | solution.py:265
  28.6 0.6 %collective-permute-start.5 = (f32[128,1024]{1,0:T(8,128)S(1)}, f32[128,1024]{1,0:T(8,128)S(1)}, u32[]{:S(2)}, u32[]{:S(2)}) collective-permute-start(f32[128,1024]{1,0:T(8,128)S(1)} %get-tuple-element.31), channel_id=1, source_target_pairs={{0,1},{1,0},{2,3},{3,2},{4,5},{5,4},{6,7},{7,6},{8,9},{9,8},{10,11... | collective-permute-start | bytes 1572872 | tf_op jit(solution)/shard_map/ppermute | solution.py:30
  29.2 0.0 collective-permute-done.7.near_ref
  29.2 1.4 %collective-permute-done.8.far_ref = bf16[128,1024]{1,0:T(8,128)(2,1)S(1)} collective-permute-done((bf16[128,1024]{1,0:T(8,128)(2,1)S(1)}, bf16[128,1024]{1,0:T(8,128)(2,1)S(1)}, u32[]{:S(2)}, u32[]{:S(2)}) %collective-permute-start.8) | collective-permute-done | bytes 262176 | tf_op jit(solution)/shard_map/ppermute | solution.py:30
  30.6 0.1 shard_map.71.refs_0_.mixed_ref
  30.7 0.0 collective-permute-done.6.theirs_ref
  30.7 0.1 shard_map.72
  30.8 1.6 %collective-permute-start.9 = (bf16[128,1024]{1,0:T(8,128)(2,1)S(1)}, bf16[128,1024]{1,0:T(8,128)(2,1)S(1)}, u32[]{:S(2)}, u32[]{:S(2)}) collective-permute-start(bf16[128,1024]{1,0:T(8,128)(2,1)S(1)} %shard_map.72), channel_id=1, source_target_pairs={{0,2},{1,3},{2,0},{3,1},{4,6},{5,7},{6,4},{7,5},{8,10},{9,11},{10,... | collective-permute-start | bytes 786440 | tf_op jit(solution)/shard_map/ppermute | solution.py:30
  32.4 0.0 copy-done
  32.4 1.6 %shard_map.73.base_ref = f32[128,1024]{1,0:T(8,128)S(1)} custom-call(bf16[256,1024]{1,0:T(8,128)(2,1)S(1)} %shard_map.71.refs_0_.mixed_ref, bf16[3,1,128,128]{3,2,1,0:T(8,128)(2,1)S(1)} %constant_dynamic-slice_fusion.w_ref), custom_call_target="tpu_custom_call" | custom-call | flops 536870912 | bytes 2097152 | tf_op jit(solution)/shard_map/pallas_call | solution.py:401
  34.0 0.0 collective-permute-done.5.near_ref
  34.0 4.4 %collective-permute-done.9.far_ref = bf16[128,1024]{1,0:T(8,128)(2,1)S(1)} collective-permute-done((bf16[128,1024]{1,0:T(8,128)(2,1)S(1)}, bf16[128,1024]{1,0:T(8,128)(2,1)S(1)}, u32[]{:S(2)}, u32[]{:S(2)}) %collective-permute-start.9) | collective-permute-done | bytes 262176 | tf_op jit(solution)/shard_map/ppermute | solution.py:30
  38.4 1.8 %shard_map.74 = f32[128,128]{1,0:T(8,128)S(1)} custom-call(f32[128,1024]{1,0:T(8,128)S(1)} %get-tuple-element.30.refs_1_.own_ref, f32[128,1024]{1,0:T(8,128)S(1)} %collective-permute-done.5.near_ref, bf16[128,1024]{1,0:T(8,128)(2,1)S(1)} %collective-permute-done.9.far_ref, bf16[3,1,128,128]{3,2,1,0:T(8,128)(2,1)S(1)} %constant_dynamic-slice_fusion.w_ref, ...), custom_call_target="tpu_custom_call" | custom-call | flops 536870912 | bytes 2097152 | tf_op jit(solution)/shard_map/pallas_call | solution.py:413
  40.2 9.6 %all_to_all.9 = f32[8,16,128]{2,1,0:T(8,128)S(1)} all-to-all(f32[8,16,128]{2,1,0:T(8,128)S(1)} %bitcast.13), channel_id=1, replica_groups=mesh['seq'=8,'mp'=4] {'seq'}, dimensions={0} | all-to-all | bytes 131072 | tf_op jit(solution)/shard_map/all_to_all | solution.py:468
  49.9 0.6 %copy.8 = f32[8,16,128]{2,1,0:T(8,128)} copy(f32[8,16,128]{2,1,0:T(8,128)S(1)} %all_to_all.9) | data formatting | bytes 131072
  (5 shorter events, 0.1 us)
Async XLA Ops:
  0.0 32.4 %copy-start = (bf16[3,8,128,128]{3,2,1,0:T(8,128)(2,1)S(1)}, bf16[3,8,128,128]{3,2,1,0:T(8,128)(2,1)}, u32[]{:S(2)}) copy-start(bf16[3,8,128,128]{3,2,1,0:T(8,128)(2,1)} %param.11) | copy-start | bytes 2359300
  0.8 5.5 %collective-permute-start = (s32[1,3,128]{2,1,0:T(4,128)S(1)}, s32[1,3,128]{2,1,0:T(4,128)S(1)}, u32[]{:S(2)}, u32[]{:S(2)}) collective-permute-start(s32[1,3,128]{2,1,0:T(4,128)S(1)} %add_bitcast_fusion), channel_id=1, source_target_pairs={{0,12},{4,8},{8,4},{12,0},{16,28},{20,24},{24,20},{28,16},{1,13},{... | collective-permute-start | bytes 4616 | tf_op jit(solution)/shard_map/ppermute | solution.py:30
  4.8 3.6 %collective-permute-start.1 = (s32[1,3,128]{2,1,0:T(4,128)S(1)}, s32[1,3,128]{2,1,0:T(4,128)S(1)}, u32[]{:S(2)}, u32[]{:S(2)}) collective-permute-start(s32[1,3,128]{2,1,0:T(4,128)S(1)} %add_bitcast_fusion), channel_id=1, source_target_pairs={{0,8},{4,12},{8,0},{12,4},{16,24},{20,28},{24,16},{28,20},{1,9},{5... | collective-permute-start | bytes 4616 | tf_op jit(solution)/shard_map/ppermute | solution.py:30
  5.2 3.6 %collective-permute-start.2 = (s32[1,3,128]{2,1,0:T(4,128)S(1)}, s32[1,3,128]{2,1,0:T(4,128)S(1)}, u32[]{:S(2)}, u32[]{:S(2)}) collective-permute-start(s32[1,3,128]{2,1,0:T(4,128)S(1)} %add_bitcast_fusion), channel_id=1, source_target_pairs={{0,4},{4,0},{8,12},{12,8},{16,20},{20,16},{24,28},{28,24},{1,5},{5... | collective-permute-start | bytes 4616 | tf_op jit(solution)/shard_map/ppermute | solution.py:30
  9.5 6.5 %collective-permute-start.3 = (s32[4,3,128]{2,1,0:T(4,128)S(1)}, s32[4,3,128]{2,1,0:T(4,128)S(1)}, u32[]{:S(2)}, u32[]{:S(2)}) collective-permute-start(s32[4,3,128]{2,1,0:T(4,128)S(1)} %pad_add_fusion.1), channel_id=1, source_target_pairs={{0,16},{4,20},{8,24},{12,28},{16,0},{20,4},{24,8},{28,12},{1,17},{... | collective-permute-start | bytes 18440 | tf_op jit(solution)/shard_map/ppermute | solution.py:30
  12.2 3.1 %copy-start.1 = (bf16[64,128]{1,0:T(8,128)(2,1)S(1)}, bf16[64,128]{1,0:T(8,128)(2,1)}, u32[]{:S(2)}) copy-start(bf16[64,128]{1,0:T(8,128)(2,1)} %_.2) | copy-start | bytes 49156
  20.2 2.0 %collective-permute-start.4 = (f32[128,1024]{1,0:T(8,128)S(1)}, f32[128,1024]{1,0:T(8,128)S(1)}, u32[]{:S(2)}, u32[]{:S(2)}) collective-permute-start(f32[128,1024]{1,0:T(8,128)S(1)} %get-tuple-element.26), channel_id=1, source_target_pairs={{0,1},{1,0},{2,3},{3,2},{4,5},{5,4},{6,7},{7,6},{8,9},{9,8},{10,11... | collective-permute-start | bytes 1572872 | tf_op jit(solution)/shard_map/ppermute | solution.py:30
  21.0 8.2 %collective-permute-start.7 = (f32[128,1024]{1,0:T(8,128)S(1)}, f32[128,1024]{1,0:T(8,128)S(1)}, u32[]{:S(2)}, u32[]{:S(2)}) collective-permute-start(f32[128,1024]{1,0:T(8,128)S(1)} %get-tuple-element.34), channel_id=1, source_target_pairs={{0,1},{1,0},{2,3},{3,2},{4,5},{5,4},{6,7},{7,6},{8,9},{9,8},{10,11... | collective-permute-start | bytes 1572872 | tf_op jit(solution)/shard_map/ppermute | solution.py:30
  22.2 8.4 %collective-permute-start.8 = (bf16[128,1024]{1,0:T(8,128)(2,1)S(1)}, bf16[128,1024]{1,0:T(8,128)(2,1)S(1)}, u32[]{:S(2)}, u32[]{:S(2)}) collective-permute-start(bf16[128,1024]{1,0:T(8,128)(2,1)S(1)} %shard_map.68._), channel_id=1, source_target_pairs={{0,2},{1,3},{2,0},{3,1},{4,6},{5,7},{6,4},{7,5},{8,10},{9,11},{10,... | collective-permute-start | bytes 786440 | tf_op jit(solution)/shard_map/ppermute | solution.py:30
  27.8 2.9 %collective-permute-start.6 = (f32[128,1024]{1,0:T(8,128)S(1)}, f32[128,1024]{1,0:T(8,128)S(1)}, u32[]{:S(2)}, u32[]{:S(2)}) collective-permute-start(f32[128,1024]{1,0:T(8,128)S(1)} %get-tuple-element.33), channel_id=1, source_target_pairs={{0,1},{1,0},{2,3},{3,2},{4,5},{5,4},{6,7},{7,6},{8,9},{9,8},{10,11... | collective-permute-start | bytes 1572872 | tf_op jit(solution)/shard_map/ppermute | solution.py:30
  28.6 5.4 %collective-permute-start.5 = (f32[128,1024]{1,0:T(8,128)S(1)}, f32[128,1024]{1,0:T(8,128)S(1)}, u32[]{:S(2)}, u32[]{:S(2)}) collective-permute-start(f32[128,1024]{1,0:T(8,128)S(1)} %get-tuple-element.31), channel_id=1, source_target_pairs={{0,1},{1,0},{2,3},{3,2},{4,5},{5,4},{6,7},{7,6},{8,9},{9,8},{10,11... | collective-permute-start | bytes 1572872 | tf_op jit(solution)/shard_map/ppermute | solution.py:30
  30.8 7.6 %collective-permute-start.9 = (bf16[128,1024]{1,0:T(8,128)(2,1)S(1)}, bf16[128,1024]{1,0:T(8,128)(2,1)S(1)}, u32[]{:S(2)}, u32[]{:S(2)}) collective-permute-start(bf16[128,1024]{1,0:T(8,128)(2,1)S(1)} %shard_map.72), channel_id=1, source_target_pairs={{0,2},{1,3},{2,0},{3,1},{4,6},{5,7},{6,4},{7,5},{8,10},{9,11},{10,... | collective-permute-start | bytes 786440 | tf_op jit(solution)/shard_map/ppermute | solution.py:30

commit v3 on v2

--- a/solution.py
+++ b/solution.py
@@ -10,7 +10,8 @@
 
 MASKED_SCORE = -1e30
 VMEM_BYTES = 24 * 1024 * 1024
-TABLES_VMEM_BYTES = 48 * 1024 * 1024
+TABLES_VMEM_BYTES = 49 * 1024 * 1024
+WEIGHTS_VMEM_BYTES = 50 * 1024 * 1024
 WHOLE = pl.BlockSpec(memory_space=pltpu.VMEM)
 IN_HBM = pl.BlockSpec(memory_space=pltpu.HBM)
 
@@ -30,15 +31,19 @@
     return lax.ppermute(value, axis, [(i, i ^ turn) for i in range(count)])
 
 
-def gather_small(block, axis):
+def gather_small(block, axis, zeros):
     index = lax.axis_index(axis)
     held = block[None]
     bits = list(range(bits_of(lax.axis_size(axis))))
+    bits = bits[1:] + bits[:1]
+    seen = []
     for group in [bits[i : i + 2] for i in range(0, len(bits), 2)]:
         pieces = []
         for turn in range(1 << len(group)):
-            mask = turn << group[0]
+            mask = sum(((turn >> place) & 1) << bit for place, bit in enumerate(group))
             pieces.append(held if turn == 0 else swap(held, axis, mask))
+        if not seen:
+            pieces = [piece + zeros for piece in pieces]
         for place, bit in enumerate(group):
             upper = ((index >> bit) & 1) == 1
             pieces = [
@@ -46,47 +51,33 @@
                 for turn in range(len(pieces))
             ]
         held = jnp.concatenate(pieces, 0)
-    return held
+        seen = group[::-1] + seen
+    tail = held.shape[1:]
+    held = held.reshape([2] * len(bits) + list(tail))
+    order = [seen.index(bit) for bit in sorted(bits, reverse=True)]
+    held = held.transpose(order + [len(bits) + d for d in range(len(tail))])
+    return held.reshape((-1,) + tail)
 
 
 def head_here(seq_count, local_heads):
     return lax.axis_index("seq") // (seq_count // local_heads)
 
 
-def tables_kernel(
-    order, local_heads, seq_count, head_dim, embed_ref, w_out_ref, table_ref, weight_ref, planes,
-    columns, plane_sems, column_sems
-):
+def tables_kernel(embed_ref, table_ref, planes, sems):
     _, vocab, channels = embed_ref.shape
     chunk = planes.shape[2]
-    head = head_here(seq_count, local_heads)
-    mp_index = lax.axis_index("mp")
-    plane_copies = []
+    copies = []
     for c in range(vocab // chunk):
         rows = pl.ds(c * chunk, chunk)
-        plane_copies.append(
+        copies.append(
             [
-                pltpu.make_async_copy(embed_ref.at[i, rows], planes.at[i, c], plane_sems.at[i, c])
+                pltpu.make_async_copy(embed_ref.at[i, rows], planes.at[i, c], sems.at[i, c])
                 for i in range(3)
             ]
         )
-    column_copies = []
-    for p, turn in enumerate(order):
-        first = pl.multiple_of(((mp_index ^ turn) * local_heads + head) * head_dim, head_dim)
-        column_copies.append(
-            pltpu.make_async_copy(
-                w_out_ref.at[:, pl.ds(first, head_dim)], columns.at[p], column_sems.at[p]
-            )
-        )
-    for copy in column_copies:
-        copy.start()
-    for trio in plane_copies:
-        for copy in trio:
+        for copy in copies[-1]:
             copy.start()
-    for p, copy in enumerate(column_copies):
-        copy.wait()
-        weight_ref[p * head_dim : (p + 1) * head_dim, :] = columns[p].T
-    for c, trio in enumerate(plane_copies):
+    for c, trio in enumerate(copies):
         for copy in trio:
             copy.wait()
         cols = slice(c * chunk, (c + 1) * chunk)
@@ -95,29 +86,65 @@
         table_ref[channels : 2 * channels, cols] = planes[0, c].T
 
 
-def make_tables(order, seq_count, local_heads, head_dim, embed_rows, w_out):
+def make_tables(embed_rows):
     _, vocab, channels = embed_rows.shape
+    chunk = 128
+    return pl.pallas_call(
+        tables_kernel,
+        out_shape=jax.ShapeDtypeStruct((2 * channels, vocab), jnp.bfloat16),
+        in_specs=[IN_HBM],
+        out_specs=WHOLE,
+        scratch_shapes=[
+            pltpu.VMEM((3, vocab // chunk, chunk, channels), jnp.bfloat16),
+            pltpu.SemaphoreType.DMA((3, vocab // chunk)),
+        ],
+        compiler_params=params(TABLES_VMEM_BYTES),
+        cost_estimate=pl.CostEstimate(
+            flops=4 * vocab * channels, bytes_accessed=8 * 1024 * 1024, transcendentals=0
+        ),
+    )(embed_rows)
+
+
+def weights_kernel(
+    order, local_heads, seq_count, head_dim, w_out_ref, weight_ref, zeros_ref, columns, sems
+):
+    head = head_here(seq_count, local_heads)
+    mp_index = lax.axis_index("mp")
+    copies = []
+    for p, turn in enumerate(order):
+        first = pl.multiple_of(((mp_index ^ turn) * local_heads + head) * head_dim, head_dim)
+        copies.append(
+            pltpu.make_async_copy(
+                w_out_ref.at[:, pl.ds(first, head_dim)], columns.at[p], sems.at[p]
+            )
+        )
+    for copy in copies:
+        copy.start()
+    zeros_ref[...] = jnp.zeros_like(zeros_ref)
+    for p, copy in enumerate(copies):
+        copy.wait()
+        weight_ref[p * head_dim : (p + 1) * head_dim, :] = columns[p].T
+
+
+def make_weights(order, seq_count, local_heads, head_dim, w_out, ids_shape):
     count = len(order)
-    chunk = 128
-    return pl.pallas_call(
-        functools.partial(tables_kernel, order, local_heads, seq_count, head_dim),
+    return pl.pallas_call(
+        functools.partial(weights_kernel, order, local_heads, seq_count, head_dim),
         out_shape=[
-            jax.ShapeDtypeStruct((2 * channels, vocab), jnp.bfloat16),
             jax.ShapeDtypeStruct((count * head_dim, w_out.shape[0]), jnp.bfloat16),
+            jax.ShapeDtypeStruct(ids_shape, jnp.int32),
         ],
-        in_specs=[IN_HBM, IN_HBM],
+        in_specs=[IN_HBM],
         out_specs=[WHOLE] * 2,
         scratch_shapes=[
-            pltpu.VMEM((3, vocab // chunk, chunk, channels), jnp.bfloat16),
             pltpu.VMEM((count, w_out.shape[0], head_dim), jnp.bfloat16),
-            pltpu.SemaphoreType.DMA((3, vocab // chunk)),
             pltpu.SemaphoreType.DMA((count,)),
         ],
-        compiler_params=params(TABLES_VMEM_BYTES),
-        cost_estimate=pl.CostEstimate(
-            flops=4 * vocab * channels, bytes_accessed=8 * 1024 * 1024, transcendentals=0
-        ),
-    )(embed_rows, w_out)
+        compiler_params=params(WEIGHTS_VMEM_BYTES),
+        cost_estimate=pl.CostEstimate(
+            flops=count * head_dim, bytes_accessed=2 * 1024 * 1024, transcendentals=0
+        ),
+    )(w_out)
 
 
 def toeplitz_kernel(filter_ref, toeplitz_ref):
@@ -158,7 +185,6 @@
     weight_ref,
     _,
     out_ref,
-    pass_ref,
     send_ref,
     feat,
     last,
@@ -201,9 +227,9 @@
             ).astype(jnp.bfloat16)
     last[...] = feat[0:channels, (blocks - 1) * taps :]
     rows = send_ref.shape[0]
-    total = jnp.dot(weight_ref[2 * rows :, :], out_ref[...], preferred_element_type=jnp.float32)
-    pass_ref[...] = total[0:rows]
-    send_ref[...] = total[rows:]
+    send_ref[...] = jnp.dot(
+        weight_ref[3 * rows :, :], out_ref[...], preferred_element_type=jnp.float32
+    )
 
 
 def tiles_of(length, taps):
@@ -230,49 +256,49 @@
         out_shape=[
             jax.ShapeDtypeStruct((channels, length), jnp.bfloat16),
             jax.ShapeDtypeStruct((head_dim, length), jnp.float32),
-            jax.ShapeDtypeStruct((head_dim, length), jnp.float32),
         ],
         grid=(steps,),
         in_specs=[WHOLE] * 5,
-        out_specs=column_specs(length, tile, (channels, head_dim, head_dim)),
+        out_specs=column_specs(length, tile, (channels, head_dim)),
         scratch_shapes=[
             pltpu.VMEM((2 * channels, tile), jnp.bfloat16),
             pltpu.VMEM((channels, taps), jnp.bfloat16),
         ],
         compiler_params=params(),
         cost_estimate=pl.CostEstimate(
-            flops=4 * length * channels * (vocab + taps) + 4 * length * channels * head_dim,
+            flops=4 * length * channels * (vocab + taps) + 2 * length * channels * head_dim,
             bytes_accessed=8 * 1024 * 1024,
             transcendentals=0,
         ),
     )(ids, table, toeplitz, weight, after)
 
 
-def project_kernel(mixed_ref, weight_ref, _, own_ref, near_ref):
+def project_kernel(mixed_ref, weight_ref, own_ref, near_ref, pass_ref):
     rows = own_ref.shape[0]
     total = jnp.dot(
-        weight_ref[0 : 2 * rows, :], mixed_ref[...], preferred_element_type=jnp.float32
+        weight_ref[0 : 3 * rows, :], mixed_ref[...], preferred_element_type=jnp.float32
     )
     own_ref[...] = total[0:rows]
-    near_ref[...] = total[rows:]
-
-
-def project(mixed, weight, taps, after):
+    near_ref[...] = total[rows : 2 * rows]
+    pass_ref[...] = total[2 * rows :]
+
+
+def project(mixed, weight, taps):
     channels, length = mixed.shape
     rows = weight.shape[0] // 4
     tile, steps = tiles_of(length, taps)
-    specs = column_specs(length, tile, (channels, rows, rows))
+    specs = column_specs(length, tile, (channels, rows, rows, rows))
     return pl.pallas_call(
         project_kernel,
-        out_shape=[jax.ShapeDtypeStruct((rows, length), jnp.float32)] * 2,
+        out_shape=[jax.ShapeDtypeStruct((rows, length), jnp.float32)] * 3,
         grid=(steps,),
-        in_specs=[specs[0], WHOLE, WHOLE],
+        in_specs=[specs[0], WHOLE],
         out_specs=specs[1:],
         compiler_params=params(),
         cost_estimate=pl.CostEstimate(
-            flops=4 * length * channels * rows, bytes_accessed=1024 * 1024, transcendentals=0
-        ),
-    )(mixed, weight, after)
+            flops=6 * length * channels * rows, bytes_accessed=1024 * 1024, transcendentals=0
+        ),
+    )(mixed, weight)
 
 
 def split(exact):
@@ -329,30 +355,37 @@
 
     queries, keys, values = project_head(0), project_head(1).T, project_head(2)
 
-    def finish(first, parts, values_seen):
+    def softmax(parts):
         top = functools.reduce(
             jnp.maximum, [jnp.max(part, axis=0, keepdims=True) for part in parts]
         )
         weights = [jnp.exp2((part - top) * scale) for part in parts]
         row_sum = sum(jnp.sum(part, axis=0, keepdims=True) for part in weights)
-        probs = jnp.concatenate([part.astype(jnp.bfloat16) for part in weights], axis=0)
-        return jnp.dot(values_seen, probs, preferred_element_type=jnp.float32) / row_sum
+        return jnp.concatenate([part.astype(jnp.bfloat16) for part in weights], axis=0), row_sum
 
     def score(keys_seen, queries_block):
         return jnp.dot(keys_seen, queries_block, preferred_element_type=jnp.float32)
 
-    if length <= 2048:
-        span = min(512, length)
+    def average(values_seen, probs, row_sum):
+        total = jnp.dot(values_seen, probs, preferred_element_type=jnp.float32)
+        return total * (1.0 / row_sum)
+
+    span = min(256, length)
+    if length <= 1024:
         row = lax.broadcasted_iota(jnp.int32, (span, span), 0)
         col = lax.broadcasted_iota(jnp.int32, (span, span), 1)
+        scores = []
         for first in range(0, length, span):
             cols = slice(first, first + span)
             parts = [jnp.where(row <= col, score(keys[cols], queries[:, cols]), MASKED_SCORE)]
             if first > 0:
                 parts = [score(keys[:first], queries[:, cols])] + parts
-            out_ref[:, cols] = finish(first, parts, values[:, : first + span])
+            scores.append(parts)
+        weighted = [softmax(parts) for parts in scores]
+        for i, (probs, row_sum) in enumerate(weighted):
+            seen = (i + 1) * span
+            out_ref[:, i * span : seen] = average(values[:, :seen], probs, row_sum)
     else:
-        span = 256
         out_ref[...] = queries.astype(jnp.float32)
 
         @pl.loop(0, length // span)
@@ -363,7 +396,7 @@
             key_pos = lax.broadcasted_iota(jnp.int32, scores.shape, 0)
             query_pos = first + lax.broadcasted_iota(jnp.int32, scores.shape, 1)
             scores = jnp.where(key_pos <= query_pos, scores, MASKED_SCORE)
-            out_ref[:, cols] = finish(first, [scores], values)
+            out_ref[:, cols] = average(values, *softmax([scores]))
 
 
 def first_kernel(mixed_ref, w_ref, out_ref):
@@ -385,7 +418,7 @@
         kept, difference, (((1,), (1,)), ((), ())), preferred_element_type=jnp.float32
     )
     count = jnp.sum(mask, axis=1, keepdims=True)
-    out_ref[...] = gram / jnp.maximum(count, 1.0)
+    out_ref[...] = gram * (1.0 / jnp.maximum(count, 1.0))
 
 
 def attention_cost(length, head_dim):
@@ -433,34 +466,30 @@
     assert token_ids.shape[1] % taps == 0
 
     packed = jnp.concatenate([token_ids, pair_mask[None]], 0)
-    table, weight = make_tables(
-        (0, 1, 2, 3),
-        seq_count,
-        local_heads,
-        head_dim,
-        jnp.transpose(embed_table, (1, 0, 2)),
-        w_out,
-    )
-    (table, weight), conv_filter = lax.optimization_barrier(((table, weight), conv_filter))
+    weight, zeros = make_weights(
+        (0, 1, 2, 3), seq_count, local_heads, head_dim, w_out, packed.shape
+    )
+    table = make_tables(jnp.transpose(embed_table, (1, 0, 2)))
+    table, conv_filter = lax.optimization_barrier((table, conv_filter))
     toeplitz = make_toeplitz(conv_filter)
-    ids = gather_small(packed, "seq")
+    ids = gather_small(packed, "seq", zeros)
     w_head = lax.dynamic_slice_in_dim(w_qkv, head_here(seq_count, local_heads), 1, 1)
     blocks_here = token_ids.shape[1] // taps
     if blocks_here > 1:
         ids = ids.reshape(seq_count, 3, blocks_here, taps).transpose(0, 2, 1, 3)
         ids = ids.reshape(seq_count * blocks_here, 3, taps)
 
-    mixed0, passed0, diagonal0 = hyena(0, group, ids, table, toeplitz, weight, conv_filter)
+    mixed0, diagonal0 = hyena(0, group, ids, table, toeplitz, weight, conv_filter)
     diagonal0 = swap(diagonal0, "mp", 1)
-    own0, near0 = project(mixed0, weight, taps, conv_filter)
-    total0 = add_parts(passed0, diagonal0, [own0])
+    own0, near0, passed0 = project(mixed0, weight, taps)
+    total0 = add_parts(passed0, diagonal0, [])
     near0 = swap(near0, "mp", 1)
     far0 = swap(total0, "mp", 2)
-    mixed1, passed1, diagonal1 = hyena(1, group, ids, table, toeplitz, weight, total0)
+    mixed1, diagonal1 = hyena(1, group, ids, table, toeplitz, weight, total0)
     diagonal1 = swap(diagonal1, "mp", 1)
-    own1, near1 = project(mixed1, weight, taps, conv_filter)
+    own1, near1, passed1 = project(mixed1, weight, taps)
     complete0 = complete(own0, near0, far0)
-    total1 = add_parts(passed1, diagonal1, [complete0, own1])
+    total1 = add_parts(passed1, diagonal1, [complete0])
     near1 = swap(near1, "mp", 1)
     far1 = swap(total1, "mp", 2)
     base = attend_first(complete0, w_head)

time: 50.7 us -> 49.4 us (0.974)
  other arithmetic: 1.5 us -> 0.82 us
  waiting for transfers between devices: 9.83 us -> 9.25 us
    select_n x2 -> x3, other arithmetic: 0.71 us -> 0.03 us  [gather_small(): jnp.where(upper, pieces[turn ^ 1 << place], pieces[turn])]
    ppermute x10, waiting for transfers between devices: 9.83 us -> 9.25 us  [swap(): return lax.ppermute(value, axis, [(i, i ^ turn) for i in range(count)])]
    pallas_call x2, Pallas kernels: 1.41 us -> 1.94 us  [project(): pl.pallas_call(project_kernel, out_shape=[jax.ShapeDtypeStruct((rows, len...]
    pallas_call x2, Pallas kernels: 8.17 us -> 7.64 us  [hyena(): pl.pallas_call(functools.partial(hyena_kernel, which, group), out_shape=[...]
    pallas_call x1 -> x2, Pallas kernels: 3.14 us -> 3.59 us  [the longest x1 2.11 us: make_tables(): pl.pallas_call(tables_kernel, out_shape=jax.ShapeDtypeStruct((2 * channel...]
  transfers between devices with their start and end apart: 10 -> 10, of which waited for: 6 -> 5; matrix products, arithmetic and copies ran while one was open for 0% -> 0% of each run, Pallas kernels for 22% -> 24%
where the time goes in v3:
time: 49.4 us; the launch traced here: 49.2 us
  Pallas kernels  17.1 us (35%)
  starting transfers between devices  11.6 us (23%)
  blocking collectives  9.54 us (19%)
  waiting for transfers between devices  9.25 us (19%)
  other arithmetic  0.82 us (2%)
  local copies, waits for them, and re-layouts  0.66 us (1%)
    ppermute x10, starting transfers between devices, swap(): return lax.ppermute(value, axis, [(i, i ^ turn) for i in range(count)])  11.6 us
    all_to_all x1, blocking collectives, body(): rows = lax.all_to_all(gram, 'seq', 0, 0, tiled=True)  9.54 us
    ppermute x10, waiting for transfers between devices, swap(): return lax.ppermute(value, axis, [(i, i ^ turn) for i in range(count)])  9.25 us
    pallas_call x2, Pallas kernels, hyena(): pl.pallas_call(functools.partial(hyena_kernel, which, group), out_shape=[...  7.64 us
    pallas_call x1, Pallas kernels, make_tables(): pl.pallas_call(tables_kernel, out_shape=jax.ShapeDtypeStruct((2 * channel...  2.11 us
    pallas_call x2, Pallas kernels, project(): pl.pallas_call(project_kernel, out_shape=[jax.ShapeDtypeStruct((rows, len...  1.94 us
    pallas_call x1, Pallas kernels, attend_second(): pl.pallas_call(second_kernel, out_shape=jax.ShapeDtypeStruct((head_dim, h...  1.61 us
    pallas_call x1, Pallas kernels, make_weights(): pl.pallas_call(functools.partial(weights_kernel, order, local_heads, seq_...  1.48 us
  transfers between devices with their start and end apart: 10, of which 5 were waited for; matrix products, arithmetic and copies ran while one was open for 0% of the time, Pallas kernels for 24%

profile of v3, /device:TPU:0, one launch (start us, length us, event | category | flops | bytes accessed | tf_op | source)
XLA Modules:
  0.0 49.2 jit_solution(12213725240684290051)
XLA Ops:
  0.0 0.0 copy-start
  0.0 0.8 %fusion.1 = s32[1,3,128]{2,1,0:T(4,128)S(1)} fusion(s32[1,128]{1,0:T(1,128)} %bitcast.52, s32[2,128]{1,0:T(2,128)} %param.6), kind=kLoop, calls=%fused_computation.11 | loop fusion | flops 384 | bytes 3072 | tf_op jit(solution)/shard_map/broadcast_in_dim | solution.py:36
  0.8 0.0 copy-start.2
  0.8 0.0 copy-start.3
  0.8 3.1 %collective-permute-start.2 = (s32[1,3,128]{2,1,0:T(4,128)S(1)}, s32[1,3,128]{2,1,0:T(4,128)S(1)}, u32[]{:S(2)}, u32[]{:S(2)}) collective-permute-start(s32[1,3,128]{2,1,0:T(4,128)S(1)} %fusion.1), channel_id=1, source_target_pairs={{0,8},{4,12},{8,0},{12,4},{16,24},{20,28},{24,16},{28,20},{1,9},{5... | collective-permute-start | bytes 4616 | tf_op jit(solution)/shard_map/ppermute | solution.py:31
  3.9 2.5 %collective-permute-start = (s32[1,3,128]{2,1,0:T(4,128)S(1)}, s32[1,3,128]{2,1,0:T(4,128)S(1)}, u32[]{:S(2)}, u32[]{:S(2)}) collective-permute-start(s32[1,3,128]{2,1,0:T(4,128)S(1)} %fusion.1), channel_id=1, source_target_pairs={{0,24},{4,28},{8,16},{12,20},{16,8},{20,12},{24,0},{28,4},{1,25},{... | collective-permute-start | bytes 4616 | tf_op jit(solution)/shard_map/ppermute | solution.py:31
  6.4 0.1 collective-permute-start.1
  6.5 1.5 %shard_map.64 = (bf16[512,1024]{1,0:T(8,128)(2,1)S(1)}, s32[3,128]{1,0:T(4,128)S(1)}) custom-call(bf16[1024,4096]{1,0:T(8,128)(2,1)} %w_out_ref.1), custom_call_target="tpu_custom_call" | custom-call | flops 512 | bytes 2097152 | tf_op jit(solution)/shard_map/pallas_call | solution.py:131
  8.0 0.0 copy-start.1
  8.0 0.0 collective-permute-done.2
  8.0 1.3 %collective-permute-done = s32[1,3,128]{2,1,0:T(4,128)S(1)} collective-permute-done((s32[1,3,128]{2,1,0:T(4,128)S(1)}, s32[1,3,128]{2,1,0:T(4,128)S(1)}, u32[]{:S(2)}, u32[]{:S(2)}) %collective-permute-start) | collective-permute-done | bytes 1568 | tf_op jit(solution)/shard_map/ppermute | solution.py:31
  9.3 1.6 %collective-permute-done.1 = s32[1,3,128]{2,1,0:T(4,128)S(1)} collective-permute-done((s32[1,3,128]{2,1,0:T(4,128)S(1)}, s32[1,3,128]{2,1,0:T(4,128)S(1)}, u32[]{:S(2)}, u32[]{:S(2)}) %collective-permute-start.1) | collective-permute-done | bytes 1568 | tf_op jit(solution)/shard_map/ppermute | solution.py:31
  10.8 0.0 copy-done.2
  10.8 0.0 copy-done.3
  10.9 1.6 %collective-permute-start.3 = (s32[4,3,128]{2,1,0:T(4,128)S(1)}, s32[4,3,128]{2,1,0:T(4,128)S(1)}, u32[]{:S(2)}, u32[]{:S(2)}) collective-permute-start(s32[4,3,128]{2,1,0:T(4,128)S(1)} %pad_add_fusion.1), channel_id=1, source_target_pairs={{0,4},{4,0},{8,12},{12,8},{16,20},{20,16},{24,28},{28,24},{1,5},{5... | collective-permute-start | bytes 18440 | tf_op jit(solution)/shard_map/ppermute | solution.py:31
  12.5 2.1 %shard_map.65.table_ref = bf16[2048,512]{1,0:T(8,128)(2,1)S(1)} custom-call(bf16[3,512,1024]{2,1,0:T(8,128)(2,1)} %bitcast.50), custom_call_target="tpu_custom_call" | custom-call | flops 2097152 | bytes 8388608 | tf_op jit(solution)/shard_map/pallas_call | solution.py:92
  14.6 0.0 copy-done.1
  14.6 0.7 %shard_map.66.toeplitz_ref = bf16[64,256,128]{2,1,0:T(8,128)(2,1)S(1)} custom-call(bf16[64,128]{1,0:T(8,128)(2,1)S(1)} %copy-done.1), custom_call_target="tpu_custom_call" | custom-call | flops 4194304 | bytes 4194304 | tf_op jit(solution)/shard_map/pallas_call | solution.py:165
  15.3 0.0 collective-permute-done.3
  15.4 3.8 %shard_map.67 = (bf16[1024,1024]{1,0:T(8,128)(2,1)S(1)}, f32[128,1024]{1,0:T(8,128)S(1)}) custom-call(s32[8,3,128]{2,1,0:T(4,128)S(1)} %bitcast.47, bf16[2048,512]{1,0:T(8,128)(2,1)S(1)} %shard_map.65.table_ref, bf16[64,256,128]{2,1,0:T(8,128)(2,1)S(1)} %shard_map.66.toeplitz_ref, bf16[512,1024]{1,0:T(8,128)(2,1)S(1)} %get-tuple-element.22.weight_ref, ...), custom_call_target="tpu_custom_call" | custom-call | flops 2952790016 | bytes 8388608 | tf_op jit(solution)/shard_map/pallas_call | solution.py:254
  19.2 0.1 collective-permute-start.4
  19.3 1.0 %shard_map.68 = (f32[128,1024]{1,0:T(8,128)S(1)}, f32[128,1024]{1,0:T(8,128)S(1)}, f32[128,1024]{1,0:T(8,128)S(1)}) custom-call(bf16[1024,1024]{1,0:T(8,128)(2,1)S(1)} %get-tuple-element.23.mixed_ref, bf16[512,1024]{1,0:T(8,128)(2,1)S(1)} %get-tuple-element.22.weight_ref), custom_call_target="tpu_custom_call" | custom-call | flops 805306368 | bytes 1048576 | tf_op jit(solution)/shard_map/pallas_call | solution.py:291
  20.3 0.6 %collective-permute-start.7 = (f32[128,1024]{1,0:T(8,128)S(1)}, f32[128,1024]{1,0:T(8,128)S(1)}, u32[]{:S(2)}, u32[]{:S(2)}) collective-permute-start(f32[128,1024]{1,0:T(8,128)S(1)} %get-tuple-element.32), channel_id=1, source_target_pairs={{0,1},{1,0},{2,3},{3,2},{4,5},{5,4},{6,7},{7,6},{8,9},{9,8},{10,11... | collective-permute-start | bytes 1572872 | tf_op jit(solution)/shard_map/ppermute | solution.py:31
  20.8 0.4 collective-permute-done.4.theirs_ref
  21.2 1.6 %collective-permute-start.8 = (bf16[128,1024]{1,0:T(8,128)(2,1)S(1)}, bf16[128,1024]{1,0:T(8,128)(2,1)S(1)}, u32[]{:S(2)}, u32[]{:S(2)}) collective-permute-start(bf16[128,1024]{1,0:T(8,128)(2,1)S(1)} %shard_map.69._), channel_id=1, source_target_pairs={{0,2},{1,3},{2,0},{3,1},{4,6},{5,7},{6,4},{7,5},{8,10},{9,11},{10,... | collective-permute-start | bytes 786440 | tf_op jit(solution)/shard_map/ppermute | solution.py:31
  22.8 3.8 %shard_map.70 = (bf16[1024,1024]{1,0:T(8,128)(2,1)S(1)}, f32[128,1024]{1,0:T(8,128)S(1)}) custom-call(s32[8,3,128]{2,1,0:T(4,128)S(1)} %bitcast.48, bf16[2048,512]{1,0:T(8,128)(2,1)S(1)} %shard_map.65.table_ref, bf16[64,256,128]{2,1,0:T(8,128)(2,1)S(1)} %shard_map.66.toeplitz_ref, bf16[512,1024]{1,0:T(8,128)(2,1)S(1)} %get-tuple-element.22.weight_ref, ...), custom_call_target="tpu_custom_call" | custom-call | flops 2952790016 | bytes 8388608 | tf_op jit(solution)/shard_map/pallas_call | solution.py:254
  26.6 0.1 collective-permute-start.6
  26.7 1.0 %shard_map.71 = (f32[128,1024]{1,0:T(8,128)S(1)}, f32[128,1024]{1,0:T(8,128)S(1)}, f32[128,1024]{1,0:T(8,128)S(1)}) custom-call(bf16[1024,1024]{1,0:T(8,128)(2,1)S(1)} %get-tuple-element.26.mixed_ref, bf16[512,1024]{1,0:T(8,128)(2,1)S(1)} %get-tuple-element.22.weight_ref), custom_call_target="tpu_custom_call" | custom-call | flops 805306368 | bytes 1048576 | tf_op jit(solution)/shard_map/pallas_call | solution.py:291
  27.7 0.6 %collective-permute-start.5 = (f32[128,1024]{1,0:T(8,128)S(1)}, f32[128,1024]{1,0:T(8,128)S(1)}, u32[]{:S(2)}, u32[]{:S(2)}) collective-permute-start(f32[128,1024]{1,0:T(8,128)S(1)} %get-tuple-element.28), channel_id=1, source_target_pairs={{0,1},{1,0},{2,3},{3,2},{4,5},{5,4},{6,7},{7,6},{8,9},{9,8},{10,11... | collective-permute-start | bytes 1572872 | tf_op jit(solution)/shard_map/ppermute | solution.py:31
  28.2 0.0 collective-permute-done.7.near_ref
  28.2 1.4 %collective-permute-done.8.far_ref = bf16[128,1024]{1,0:T(8,128)(2,1)S(1)} collective-permute-done((bf16[128,1024]{1,0:T(8,128)(2,1)S(1)}, bf16[128,1024]{1,0:T(8,128)(2,1)S(1)}, u32[]{:S(2)}, u32[]{:S(2)}) %collective-permute-start.8) | collective-permute-done | bytes 262176 | tf_op jit(solution)/shard_map/ppermute | solution.py:31
  29.6 0.1 shard_map.72.refs_0_.mixed_ref
  29.8 0.0 collective-permute-done.6.theirs_ref
  29.8 0.1 shard_map.73
  29.8 1.6 %collective-permute-start.9 = (bf16[128,1024]{1,0:T(8,128)(2,1)S(1)}, bf16[128,1024]{1,0:T(8,128)(2,1)S(1)}, u32[]{:S(2)}, u32[]{:S(2)}) collective-permute-start(bf16[128,1024]{1,0:T(8,128)(2,1)S(1)} %shard_map.73), channel_id=1, source_target_pairs={{0,2},{1,3},{2,0},{3,1},{4,6},{5,7},{6,4},{7,5},{8,10},{9,11},{10,... | collective-permute-start | bytes 786440 | tf_op jit(solution)/shard_map/ppermute | solution.py:31
  31.4 0.0 copy-done
  31.4 1.4 %shard_map.74.base_ref = f32[128,1024]{1,0:T(8,128)S(1)} custom-call(bf16[256,1024]{1,0:T(8,128)(2,1)S(1)} %shard_map.72.refs_0_.mixed_ref, bf16[3,1,128,128]{3,2,1,0:T(8,128)(2,1)S(1)} %constant_dynamic-slice_fusion.w_ref), custom_call_target="tpu_custom_call" | custom-call | flops 536870912 | bytes 2097152 | tf_op jit(solution)/shard_map/pallas_call | solution.py:434
  32.8 0.0 collective-permute-done.5.near_ref
  32.8 4.6 %collective-permute-done.9.far_ref = bf16[128,1024]{1,0:T(8,128)(2,1)S(1)} collective-permute-done((bf16[128,1024]{1,0:T(8,128)(2,1)S(1)}, bf16[128,1024]{1,0:T(8,128)(2,1)S(1)}, u32[]{:S(2)}, u32[]{:S(2)}) %collective-permute-start.9) | collective-permute-done | bytes 262176 | tf_op jit(solution)/shard_map/ppermute | solution.py:31
  37.4 1.6 %shard_map.75 = f32[128,128]{1,0:T(8,128)S(1)} custom-call(f32[128,1024]{1,0:T(8,128)S(1)} %get-tuple-element.27.own_ref, f32[128,1024]{1,0:T(8,128)S(1)} %collective-permute-done.5.near_ref, bf16[128,1024]{1,0:T(8,128)(2,1)S(1)} %collective-permute-done.9.far_ref, bf16[3,1,128,128]{3,2,1,0:T(8,128)(2,1)S(1)} %constant_dynamic-slice_fusion.w_ref, ...), custom_call_target="tpu_custom_call" | custom-call | flops 536870912 | bytes 2097152 | tf_op jit(solution)/shard_map/pallas_call | solution.py:446
  39.0 9.5 %all_to_all.9 = f32[8,16,128]{2,1,0:T(8,128)S(1)} all-to-all(f32[8,16,128]{2,1,0:T(8,128)S(1)} %bitcast.46), channel_id=1, replica_groups=mesh['seq'=8,'mp'=4] {'seq'}, dimensions={0} | all-to-all | bytes 131072 | tf_op jit(solution)/shard_map/all_to_all | solution.py:497
  48.6 0.6 %copy.9 = f32[8,16,128]{2,1,0:T(8,128)} copy(f32[8,16,128]{2,1,0:T(8,128)S(1)} %all_to_all.9) | data formatting | bytes 131072
  (8 shorter events, 0.1 us)
Async XLA Ops:
  0.0 31.4 %copy-start = (bf16[3,8,128,128]{3,2,1,0:T(8,128)(2,1)S(1)}, bf16[3,8,128,128]{3,2,1,0:T(8,128)(2,1)}, u32[]{:S(2)}) copy-start(bf16[3,8,128,128]{3,2,1,0:T(8,128)(2,1)} %param.11) | copy-start | bytes 2359300
  0.8 10.1 %copy-start.2 = (s32[2,128]{1,0:T(2,128)S(1)}, s32[2,128]{1,0:T(2,128)}, u32[]{:S(2)}) copy-start(s32[2,128]{1,0:T(2,128)} %param.6) | copy-start | bytes 3076
  0.8 10.1 %copy-start.3 = (s32[128]{0:T(128)S(1)}, s32[128]{0:T(128)}, u32[]{:S(2)}) copy-start(s32[128]{0:T(128)} %param.7) | copy-start | bytes 1540
  0.8 7.2 %collective-permute-start.2 = (s32[1,3,128]{2,1,0:T(4,128)S(1)}, s32[1,3,128]{2,1,0:T(4,128)S(1)}, u32[]{:S(2)}, u32[]{:S(2)}) collective-permute-start(s32[1,3,128]{2,1,0:T(4,128)S(1)} %fusion.1), channel_id=1, source_target_pairs={{0,8},{4,12},{8,0},{12,4},{16,24},{20,28},{24,16},{28,20},{1,9},{5... | collective-permute-start | bytes 4616 | tf_op jit(solution)/shard_map/ppermute | solution.py:31
  3.9 5.4 %collective-permute-start = (s32[1,3,128]{2,1,0:T(4,128)S(1)}, s32[1,3,128]{2,1,0:T(4,128)S(1)}, u32[]{:S(2)}, u32[]{:S(2)}) collective-permute-start(s32[1,3,128]{2,1,0:T(4,128)S(1)} %fusion.1), channel_id=1, source_target_pairs={{0,24},{4,28},{8,16},{12,20},{16,8},{20,12},{24,0},{28,4},{1,25},{... | collective-permute-start | bytes 4616 | tf_op jit(solution)/shard_map/ppermute | solution.py:31
  6.4 4.5 %collective-permute-start.1 = (s32[1,3,128]{2,1,0:T(4,128)S(1)}, s32[1,3,128]{2,1,0:T(4,128)S(1)}, u32[]{:S(2)}, u32[]{:S(2)}) collective-permute-start(s32[1,3,128]{2,1,0:T(4,128)S(1)} %fusion.1), channel_id=1, source_target_pairs={{0,16},{4,20},{8,24},{12,28},{16,0},{20,4},{24,8},{28,12},{1,17},{... | collective-permute-start | bytes 4616 | tf_op jit(solution)/shard_map/ppermute | solution.py:31
  8.0 6.6 %copy-start.1 = (bf16[64,128]{1,0:T(8,128)(2,1)S(1)}, bf16[64,128]{1,0:T(8,128)(2,1)}, u32[]{:S(2)}) copy-start(bf16[64,128]{1,0:T(8,128)(2,1)} %_) | copy-start | bytes 49156
  10.9 4.4 %collective-permute-start.3 = (s32[4,3,128]{2,1,0:T(4,128)S(1)}, s32[4,3,128]{2,1,0:T(4,128)S(1)}, u32[]{:S(2)}, u32[]{:S(2)}) collective-permute-start(s32[4,3,128]{2,1,0:T(4,128)S(1)} %pad_add_fusion.1), channel_id=1, source_target_pairs={{0,4},{4,0},{8,12},{12,8},{16,20},{20,16},{24,28},{28,24},{1,5},{5... | collective-permute-start | bytes 18440 | tf_op jit(solution)/shard_map/ppermute | solution.py:31
  19.2 2.0 %collective-permute-start.4 = (f32[128,1024]{1,0:T(8,128)S(1)}, f32[128,1024]{1,0:T(8,128)S(1)}, u32[]{:S(2)}, u32[]{:S(2)}) collective-permute-start(f32[128,1024]{1,0:T(8,128)S(1)} %get-tuple-element.25), channel_id=1, source_target_pairs={{0,1},{1,0},{2,3},{3,2},{4,5},{5,4},{6,7},{7,6},{8,9},{9,8},{10,11... | collective-permute-start | bytes 1572872 | tf_op jit(solution)/shard_map/ppermute | solution.py:31
  20.3 8.0 %collective-permute-start.7 = (f32[128,1024]{1,0:T(8,128)S(1)}, f32[128,1024]{1,0:T(8,128)S(1)}, u32[]{:S(2)}, u32[]{:S(2)}) collective-permute-start(f32[128,1024]{1,0:T(8,128)S(1)} %get-tuple-element.32), channel_id=1, source_target_pairs={{0,1},{1,0},{2,3},{3,2},{4,5},{5,4},{6,7},{7,6},{8,9},{9,8},{10,11... | collective-permute-start | bytes 1572872 | tf_op jit(solution)/shard_map/ppermute | solution.py:31
  21.2 8.4 %collective-permute-start.8 = (bf16[128,1024]{1,0:T(8,128)(2,1)S(1)}, bf16[128,1024]{1,0:T(8,128)(2,1)S(1)}, u32[]{:S(2)}, u32[]{:S(2)}) collective-permute-start(bf16[128,1024]{1,0:T(8,128)(2,1)S(1)} %shard_map.69._), channel_id=1, source_target_pairs={{0,2},{1,3},{2,0},{3,1},{4,6},{5,7},{6,4},{7,5},{8,10},{9,11},{10,... | collective-permute-start | bytes 786440 | tf_op jit(solution)/shard_map/ppermute | solution.py:31
  26.6 3.2 %collective-permute-start.6 = (f32[128,1024]{1,0:T(8,128)S(1)}, f32[128,1024]{1,0:T(8,128)S(1)}, u32[]{:S(2)}, u32[]{:S(2)}) collective-permute-start(f32[128,1024]{1,0:T(8,128)S(1)} %get-tuple-element.30), channel_id=1, source_target_pairs={{0,1},{1,0},{2,3},{3,2},{4,5},{5,4},{6,7},{7,6},{8,9},{9,8},{10,11... | collective-permute-start | bytes 1572872 | tf_op jit(solution)/shard_map/ppermute | solution.py:31
  27.7 5.1 %collective-permute-start.5 = (f32[128,1024]{1,0:T(8,128)S(1)}, f32[128,1024]{1,0:T(8,128)S(1)}, u32[]{:S(2)}, u32[]{:S(2)}) collective-permute-start(f32[128,1024]{1,0:T(8,128)S(1)} %get-tuple-element.28), channel_id=1, source_target_pairs={{0,1},{1,0},{2,3},{3,2},{4,5},{5,4},{6,7},{7,6},{8,9},{9,8},{10,11... | collective-permute-start | bytes 1572872 | tf_op jit(solution)/shard_map/ppermute | solution.py:31
  29.8 7.6 %collective-permute-start.9 = (bf16[128,1024]{1,0:T(8,128)(2,1)S(1)}, bf16[128,1024]{1,0:T(8,128)(2,1)S(1)}, u32[]{:S(2)}, u32[]{:S(2)}) collective-permute-start(bf16[128,1024]{1,0:T(8,128)(2,1)S(1)} %shard_map.73), channel_id=1, source_target_pairs={{0,2},{1,3},{2,0},{3,1},{4,6},{5,7},{6,4},{7,5},{8,10},{9,11},{10,... | collective-permute-start | bytes 786440 | tf_op jit(solution)/shard_map/ppermute | solution.py:31
